TPU v7x, 128 devices: a whole 4x4x4 slice. The times are simulated.
128 devices in a mesh: bx: 16 (over z, x), by: 8 (over y, core).
Axes of the slice: x: 4, y: 4, z: 4, core: 2. Of those that a mesh axis runs over, the one named last changes fastest.
Arguments:
- coefficients: float32 [2, 6, 1024, 6, 1024], P(None, None, 'bx', None, 'by'), may hold values from -0.4 to 0.4
- slowness: float32 [4, 96, 96], replicated, may hold values from 0.25 to 1
Outputs:
- transformed: float32 [2, 6, 1024, 6, 1024], P(None, None, 'bx', None, 'by')
All inputs are finite; a program needn't handle non-finite values.
Results may differ from a plain program's by a relative error of at most 0.00095.
Values sent between devices are 32-bit elements; how exact they have to be, the bound alone decides.
A program may use at most 192 MiB of HBM per device.

v0:
```python
import math

import jax
import jax.numpy as jnp
import numpy as np
from jax import lax
from jax.sharding import PartitionSpec as P

N = 2048
LEVELS = 4


def partner(block, axis, stride):
    count = lax.axis_size(axis)
    route = []
    for low in range(count):
        high = low | 1 << stride
        if high != low and high < count:
            route += [(low, high), (high, low)]
    return lax.ppermute(block, axis, route)


def cheb_points_of(order_count):
    return np.cos(np.pi * (2 * np.arange(order_count) + 1) / (2 * order_count))


def lagrange_table(order_count):
    cheb_points = cheb_points_of(order_count)
    weights = np.zeros((2, order_count, order_count))
    for quadrant in range(2):
        shifted = quadrant - 0.5 + cheb_points / 2
        for target in range(order_count):
            for source in range(order_count):
                product = 1.0
                for others in range(order_count):
                    if others != source:
                        product = (
                            product
                            * (shifted[target] - cheb_points[others])
                            / (cheb_points[source] - cheb_points[others])
                        )
                weights[quadrant, target, source] = product
    return weights


def row_terms(row_ids, total_bits, level_index, grid_size, order_count):
    shift_bits = total_bits - level_index
    parent_box = row_ids >> shift_bits
    child_bit = row_ids >> shift_bits - 1 & 1
    source_box = jnp.zeros_like(row_ids)
    for offset in range(shift_bits):
        source_box = source_box + (row_ids >> shift_bits - 1 - offset & 1) * (1 << offset)
    box_width = grid_size * 2.0**level_index / 2.0**total_bits
    child_freq = (source_box.astype(jnp.float32) + 0.5) * box_width - grid_size / 2.0
    parent_freq = child_freq - (child_bit.astype(jnp.float32) - 0.5) * box_width
    cheb_points = jnp.asarray(cheb_points_of(order_count), jnp.float32)
    quadrants = jnp.arange(2, dtype=jnp.int32)
    target_box = 2 * parent_box[None, :] + quadrants[:, None]
    position = (
        target_box[:, None, :].astype(jnp.float32) + (1.0 + cheb_points)[None, :, None] / 2.0
    ) / 2.0 ** (level_index + 1)
    lookup = (
        order_count * target_box[:, None, :]
        + jnp.arange(order_count, dtype=jnp.int32)[None, :, None]
    )
    return (position, child_freq, parent_freq, lookup)


def row_split(local_rows, local_level, remote):
    if remote:
        return (1, 1, local_rows)
    high_part = 2**local_level
    return (high_part, 2, local_rows // (2 * high_part))


def own_bit_of(position, level_index, dev_bits):
    return position >> dev_bits - 1 - level_index & 1


def trade_x(terms, level_index, dev_bits):
    own_bit = own_bit_of(lax.axis_index("bx"), level_index, dev_bits)
    kept_half = lax.dynamic_index_in_dim(terms, own_bit, 1, keepdims=False)
    sent_half = lax.dynamic_index_in_dim(terms, 1 - own_bit, 1, keepdims=False)
    return kept_half + partner(sent_half, "bx", dev_bits - 1 - level_index)


def trade_y(terms, level_index, dev_bits, quad_axis):
    own_bit = own_bit_of(lax.axis_index("by"), level_index, dev_bits)
    kept_half = lax.dynamic_index_in_dim(terms, own_bit, quad_axis, keepdims=False)
    sent_half = lax.dynamic_index_in_dim(terms, 1 - own_bit, quad_axis, keepdims=False)
    return kept_half + partner(sent_half, "by", dev_bits - 1 - level_index)


def shards(coefficients, slowness):
    highest = lax.Precision.HIGHEST
    order_count = coefficients.shape[1]
    local_x = coefficients.shape[2]
    local_y = coefficients.shape[4]
    size_x = lax.axis_size("bx")
    size_y = lax.axis_size("by")
    dev_bits_x = size_x.bit_length() - 1
    dev_bits_y = size_y.bit_length() - 1
    total_x = (local_x * size_x).bit_length() - 1
    total_y = (local_y * size_y).bit_length() - 1
    rows_x = lax.axis_index("bx") * local_x + lax.iota(jnp.int32, local_x)
    rows_y = lax.axis_index("by") * local_y + lax.iota(jnp.int32, local_y)
    columns = lax.iota(jnp.int32, slowness.shape[1])
    lagrange = jnp.asarray(lagrange_table(order_count), jnp.float32)
    current = coefficients
    for level_index in range(LEVELS):
        remote_y = level_index < dev_bits_y
        pos_x, child_x, parent_x, look_x = row_terms(rows_x, total_x, level_index, N, order_count)
        pos_y, child_y, parent_y, look_y = row_terms(rows_y, total_y, level_index, N, order_count)
        step_x = child_x - parent_x
        step_y = child_y - parent_y
        magnitude = jnp.sqrt(child_x[:, None] ** 2 + child_y[None, :] ** 2) - jnp.sqrt(
            parent_x[:, None] ** 2 + parent_y[None, :] ** 2
        )
        hot_x = (look_x.reshape(-1)[:, None] == columns[None, :]).astype(jnp.float32)
        hot_y = (look_y.reshape(-1)[:, None] == columns[None, :]).astype(jnp.float32)
        speed_vals = jnp.dot(
            jnp.dot(hot_x, slowness[level_index], precision=highest), hot_y.T, precision=highest
        )
        speed_vals = speed_vals.reshape(2, order_count, local_x, 2, order_count, local_y)
        angles = (
            pos_x[:, :, :, None, None, None] * step_x[None, None, :, None, None, None]
            + pos_y[None, None, None, :, :, :] * step_y[None, None, None, None, None, :]
            + speed_vals * magnitude[None, None, :, None, None, :]
        )
        angles = 2.0 * math.pi * angles
        interp = jnp.einsum("qts,zsaub->zqtaub", lagrange, current, precision=highest)
        interp = jnp.einsum("puv,zqtavb->zqtapub", lagrange, interp, precision=highest)
        cosine = jnp.cos(angles)
        sine_part = jnp.sin(angles)
        real_part = cosine * interp[0] - sine_part * interp[1]
        imag_part = cosine * interp[1] + sine_part * interp[0]
        terms = jnp.stack([real_part, imag_part])
        level_remote_x = level_index < dev_bits_x
        level_remote_y = level_index < dev_bits_y
        split_x = row_split(local_x, level_index - dev_bits_x, level_remote_x)
        split_y = row_split(local_y, level_index - dev_bits_y, level_remote_y)
        terms = terms.reshape((2, 2, order_count) + split_x + (2, order_count) + split_y)
        spec_x = "abce"
        spec_y = "fghj" if level_remote_y else "ghfj"
        terms = jnp.einsum("zabcdefghij->z" + spec_x + spec_y, terms)
        terms = trade_x(terms, level_index, dev_bits_x)
        if remote_y:
            terms = trade_y(terms, level_index, dev_bits_y, 4)
        current = terms.reshape(2, order_count, local_x, order_count, local_y)
    return current


def solution(mesh):
    placed = (P(None, None, "bx", None, "by"), P())
    return jax.shard_map(
        shards,
        mesh=mesh,
        in_specs=placed,
        out_specs=P(None, None, "bx", None, "by"),
        check_vma=False,
    )
```

profile of v0, /device:TPU:1, one launch (start us, length us, event | category | flops | bytes accessed | tf_op | source)
XLA Modules:
  0.0 873.2 jit_solution(5420266570539047933)
XLA Ops:
  6.2 7.2 reshape.1439
  13.4 7.3 fusion.43
  20.8 12.4 %fusion.22 = f32[2,2,6,64,2,6,128]{6,5,4,3,2,1,0:T(8,128)} fusion(f32[2,6,6,1,1,1,1]{2,1,0,6,5,4,3:T(8,128)S(1)} %copy-done.5, f32[2,2,6,64,6,128,1]{5,2,4,3,0,1,6:T(8,128)S(1)} %fusion.43), kind=kOutput, calls=%fused_computation.55 | convolution fusion | flops 169869312 | bytes 14156064 | tf_op jit(solution)/shard_map/puv,zqtavb->zqtapub/dot_general | solution.py:132
  33.4 28.6 %multiply_add_fusion.3 = (f32[1,2,6,64,2,6,128]{6,5,4,3,2,1,0:T(8,128)S(1)}, f32[1,2,6,64,2,6,128]{6,5,4,3,2,1,0:T(8,128)S(1)}) fusion(f32[2,2,6,64,2,6,128]{6,5,4,3,2,1,0:T(8,128)} %fusion.22, f32[1,2,6,64,2,6,128]{6,5,4,3,2,1,0:T(8,128)} %reshape.1439, f32[64,128]{1,0:T(8,128)S(1)} %sqrt_subtract_fusion, f32[2,6,128]{2,1,0:T(8,128)S(1)} %get-tuple-element.28, ...), kind=kLoop, calls=%fused_computation.33 | loop fusion | flops 11796480 | bytes 23634944 | tf_op jit(solution)/shard_map/add | solution.py:136
  73.6 101.8 %collective-permute-done = f32[2,6,1,64,2,6,1,128]{7,3,6,5,4,2,1,0:T(8,128)} collective-permute-done((f32[2,6,1,64,2,6,1,128]{7,3,6,5,4,2,1,0:T(8,128)}, f32[2,6,1,64,2,6,1,128]{7,3,6,5,4,2,1,0:T(8,128)}, u32[]{:S(2)}, u32[]{:S(2)}) %collective-permute-start) | collective-permute-done | bytes 4718624 | tf_op jit(solution)/shard_map/ppermute | solution.py:20
  193.2 7.3 reshape.1438
  200.7 37.8 %collective-permute-done.1 = f32[2,6,1,64,6,1,128]{6,3,5,4,2,1,0:T(8,128)S(1)} collective-permute-done((f32[2,6,1,64,6,1,128]{6,3,5,4,2,1,0:T(8,128)}, f32[2,6,1,64,6,1,128]{6,3,5,4,2,1,0:T(8,128)S(1)}, u32[]{:S(2)}, u32[]{:S(2)}) %collective-permute-start.1) | collective-permute-done | bytes 2359328 | tf_op jit(solution)/shard_map/ppermute | solution.py:20
  240.6 6.6 fusion.46
  247.2 11.9 %fusion.25 = f32[2,2,6,64,2,6,128]{6,5,4,3,2,1,0:T(8,128)S(1)} fusion(f32[2,6,6,1,1,1,1]{2,1,0,6,5,4,3:T(8,128)S(1)} %copy-done.5, f32[2,2,6,64,6,128,1]{5,2,1,4,3,0,6:T(8,128)S(1)} %fusion.46), kind=kOutput, calls=%fused_computation.56 | convolution fusion | flops 169869312 | bytes 14156064 | tf_op jit(solution)/shard_map/puv,zqtavb->zqtapub/dot_general | solution.py:132
  259.1 25.4 %multiply_add_fusion.2 = (f32[1,2,6,64,2,6,128]{6,5,4,3,2,1,0:T(8,128)S(1)}, f32[1,2,6,64,2,6,128]{6,5,4,3,2,1,0:T(8,128)S(1)}) fusion(f32[2,2,6,64,2,6,128]{6,5,4,3,2,1,0:T(8,128)S(1)} %fusion.25, f32[1,2,6,64,2,6,128]{6,5,4,3,2,1,0:T(8,128)S(1)} %bitcast.131, f32[64,128]{1,0:T(8,128)S(1)} %sqrt_subtract_fusion.1, f32[2,6,128]{2,1,0:T(8,128)S(1)} %get-tuple-element.27, ...), kind=kLoop, calls=%fused_computation.31 | loop fusion | flops 11796480 | bytes 23634944 | tf_op jit(solution)/shard_map/add | solution.py:136
  291.7 101.1 %collective-permute-done.2 = f32[2,6,1,64,2,6,1,128]{7,3,6,5,4,2,1,0:T(8,128)} collective-permute-done((f32[2,6,1,64,2,6,1,128]{7,3,6,5,4,2,1,0:T(8,128)}, f32[2,6,1,64,2,6,1,128]{7,3,6,5,4,2,1,0:T(8,128)}, u32[]{:S(2)}, u32[]{:S(2)}) %collective-permute-start.2) | collective-permute-done | bytes 4718624 | tf_op jit(solution)/shard_map/ppermute | solution.py:20
  408.9 7.3 reshape.1437
  416.4 36.1 %collective-permute-done.3 = f32[2,6,1,64,6,1,128]{6,3,5,4,2,1,0:T(8,128)S(1)} collective-permute-done((f32[2,6,1,64,6,1,128]{6,3,5,4,2,1,0:T(8,128)}, f32[2,6,1,64,6,1,128]{6,3,5,4,2,1,0:T(8,128)S(1)}, u32[]{:S(2)}, u32[]{:S(2)}) %collective-permute-start.3) | collective-permute-done | bytes 2359328 | tf_op jit(solution)/shard_map/ppermute | solution.py:20
  461.2 11.9 %fusion.28 = f32[2,2,6,64,2,6,128]{6,5,4,3,2,1,0:T(8,128)S(1)} fusion(f32[2,6,6,1,1,1,1]{2,1,0,6,5,4,3:T(8,128)S(1)} %copy-done.5, f32[2,2,6,64,6,128,1]{5,2,1,4,3,0,6:T(8,128)S(1)} %fusion.49), kind=kOutput, calls=%fused_computation.57 | convolution fusion | flops 169869312 | bytes 14156064 | tf_op jit(solution)/shard_map/puv,zqtavb->zqtapub/dot_general | solution.py:132
  473.1 25.4 %multiply_add_fusion.1 = (f32[1,2,6,64,2,6,128]{6,5,4,3,2,1,0:T(8,128)S(1)}, f32[1,2,6,64,2,6,128]{6,5,4,3,2,1,0:T(8,128)S(1)}) fusion(f32[2,2,6,64,2,6,128]{6,5,4,3,2,1,0:T(8,128)S(1)} %fusion.28, f32[1,2,6,64,2,6,128]{6,5,4,3,2,1,0:T(8,128)S(1)} %bitcast.133, f32[64,128]{1,0:T(8,128)S(1)} %sqrt_subtract_fusion.2, f32[2,6,128]{2,1,0:T(8,128)S(1)} %get-tuple-element.26, ...), kind=kLoop, calls=%fused_computation.29 | loop fusion | flops 11796480 | bytes 23634944 | tf_op jit(solution)/shard_map/add | solution.py:136
  508.0 98.4 %collective-permute-done.4 = f32[2,6,1,64,2,6,1,128]{7,3,6,5,4,2,1,0:T(8,128)} collective-permute-done((f32[2,6,1,64,2,6,1,128]{7,3,6,5,4,2,1,0:T(8,128)}, f32[2,6,1,64,2,6,1,128]{7,3,6,5,4,2,1,0:T(8,128)}, u32[]{:S(2)}, u32[]{:S(2)}) %collective-permute-start.4) | collective-permute-done | bytes 4718624 | tf_op jit(solution)/shard_map/ppermute | solution.py:20
  626.2 7.3 reshape.1436
  635.8 6.6 fusion.52
  642.4 11.9 %fusion.31 = f32[2,2,6,64,2,6,128]{6,5,4,3,2,1,0:T(8,128)S(1)} fusion(f32[2,6,6,1,1,1,1]{2,1,0,6,5,4,3:T(8,128)S(1)} %copy-done.5, f32[2,2,6,64,6,128,1]{5,2,1,4,3,0,6:T(8,128)S(1)} %fusion.52), kind=kOutput, calls=%fused_computation.58 | convolution fusion | flops 169869312 | bytes 14156064 | tf_op jit(solution)/shard_map/puv,zqtavb->zqtapub/dot_general | solution.py:132
  654.3 26.2 %multiply_subtract_fusion = (f32[1,2,6,64,2,6,128]{6,5,4,3,2,1,0:T(8,128)S(1)}, f32[1,2,6,64,2,6,128]{6,5,4,3,2,1,0:T(8,128)}) fusion(f32[2,2,6,64,2,6,128]{6,5,4,3,2,1,0:T(8,128)S(1)} %fusion.31, f32[1,2,6,64,2,6,128]{6,5,4,3,2,1,0:T(8,128)S(1)} %bitcast.129, f32[64,128]{1,0:T(8,128)S(1)} %sqrt_subtract_fusion.3, f32[2,6,128]{2,1,0:T(8,128)S(1)} %get-tuple-element.25, ...), kind=kLoop, calls=%fused_computation.28 | loop fusion | flops 11796480 | bytes 23634944 | tf_op jit(solution)/shard_map/sub | solution.py:135
  684.0 10.3 %stack.27 = f32[1,2,6,1,1,64,2,6,1,2,64]{10,9,5,7,6,2,1,8,4,3,0:T(2,128)} reshape(f32[1,2,6,64,2,6,128]{6,3,5,4,2,1,0:T(8,128)} %copy.55) | data formatting | bytes 9437184 | tf_op jit(solution)/shard_map/stack | solution.py:137
  700.7 10.1 %stack.28 = f32[1,2,6,1,1,64,2,6,1,2,64]{10,9,5,7,6,2,1,8,4,3,0:T(2,128)} reshape(f32[1,2,6,64,2,6,128]{6,3,5,4,2,1,0:T(8,128)} %copy.56) | data formatting | bytes 9437184 | tf_op jit(solution)/shard_map/stack | solution.py:137
  710.9 36.1 %maximum_reduce_fusion = f32[2,2,6,64,2,6,64]{6,3,5,4,2,1,0:T(8,128)} fusion(f32[1,2,6,1,1,64,2,6,1,2,64]{10,9,5,7,6,2,1,8,4,3,0:T(2,128)} %stack.28, f32[1,2,6,1,1,64,2,6,1,2,64]{10,9,5,7,6,2,1,8,4,3,0:T(2,128)} %stack.27), kind=kLoop, calls=%fused_computation | loop fusion | flops 3538944 | bytes 14155776 | tf_op jit(solution)/shard_map/zabcdefghij->zabceghfj/reduce_sum | solution.py:145
  753.5 102.5 %collective-permute-done.6 = f32[2,6,1,64,6,1,2,64]{7,3,4,6,1,0,5,2:T(8,128)} collective-permute-done((f32[2,6,1,64,6,1,2,64]{7,3,4,6,1,0,5,2:T(8,128)}, f32[2,6,1,64,6,1,2,64]{7,3,4,6,1,0,5,2:T(8,128)}, u32[]{:S(2)}, u32[]{:S(2)}) %collective-permute-start.6) | collective-permute-done | bytes 2359328 | tf_op jit(solution)/shard_map/ppermute | solution.py:20
  (117 shorter events, 135.1 us)
Async XLA Ops:
  6.2 7.2 copy-start.3
  6.2 7.2 copy-start.7
  13.4 7.3 copy-start.5
  20.8 12.5 %copy-start.8 = (f32[6]{0:T(128)S(1)}, f32[6]{0:T(128)}, u32[]{:S(2)}) copy-start(f32[6]{0:T(128)} %constant.198) | copy-start | bytes 76
  69.1 106.3 %collective-permute-start = (f32[2,6,1,64,2,6,1,128]{7,3,6,5,4,2,1,0:T(8,128)}, f32[2,6,1,64,2,6,1,128]{7,3,6,5,4,2,1,0:T(8,128)}, u32[]{:S(2)}, u32[]{:S(2)}) collective-permute-start(f32[2,6,1,64,2,6,1,128]{7,3,6,5,4,2,1,0:T(8,128)} %bitcast.127), channel_id=1, source_target_pairs={{0,64},{64,0},{8,72},{72,8},{16,80},{80,16},{24,88},{88,24},{32,96... | collective-permute-start | bytes 14155784 | tf_op jit(solution)/shard_map/ppermute | solution.py:20
  175.4 12.8 %copy-start.4 = (f32[4,96,96]{2,1,0:T(8,128)S(1)}, f32[4,96,96]{2,1,0:T(8,128)}, u32[]{:S(2)}) copy-start(f32[4,96,96]{2,1,0:T(8,128)} %param.12) | copy-start | bytes 442372
  181.5 2.2 copy-start
  185.2 53.2 %collective-permute-start.1 = (f32[2,6,1,64,6,1,128]{6,3,5,4,2,1,0:T(8,128)}, f32[2,6,1,64,6,1,128]{6,3,5,4,2,1,0:T(8,128)S(1)}, u32[]{:S(2)}, u32[]{:S(2)}) collective-permute-start(f32[2,6,1,64,6,1,128]{6,3,5,4,2,1,0:T(8,128)} %dynamic-slice_bitcast_fusion.3), channel_id=1, source_target_pairs={{0,4},{4,0},{1,5},{5,1},{2,6},{6,2},{3,7},{7,3},{8,12},{12,8},{9,1... | collective-permute-start | bytes 7077896 | tf_op jit(solution)/shard_map/ppermute | solution.py:20
  200.5 40.1 %copy-start.6 = (f32[2,6,6,1,1,1]{2,1,0,5,4,3:T(8,128)S(1)}, f32[2,6,6,1,1,1]{2,1,0,5,4,3:T(8,128)}, u32[]{:S(2)}) copy-start(f32[2,6,6,1,1,1]{2,1,0,5,4,3:T(8,128)} %constant.201) | copy-start | bytes 868
  240.6 18.5 %slice-start.2 = ((s8[6291456]{0:T(1024)(128)(4,1)}), s8[4194304]{0:T(1024)(128)(4,1)S(1)}, s32[]{:S(2)}) async-start(s8[6291456]{0:T(1024)(128)(4,1)} %bitcast.130), calls=%async_computation.2 | async-start | bytes 8388608
  247.2 11.9 %slice-start.3 = ((s8[6291456]{0:T(1024)(128)(4,1)}), s8[2097152]{0:T(1024)(128)(4,1)S(1)}, s32[]{:S(2)}) async-start(s8[6291456]{0:T(1024)(128)(4,1)} %bitcast.130), calls=%async_computation.3 | async-start | bytes 4194304
  291.3 101.5 %collective-permute-start.2 = (f32[2,6,1,64,2,6,1,128]{7,3,6,5,4,2,1,0:T(8,128)}, f32[2,6,1,64,2,6,1,128]{7,3,6,5,4,2,1,0:T(8,128)}, u32[]{:S(2)}, u32[]{:S(2)}) collective-permute-start(f32[2,6,1,64,2,6,1,128]{7,3,6,5,4,2,1,0:T(8,128)} %bitcast.126), channel_id=1, source_target_pairs={{0,32},{32,0},{8,40},{40,8},{16,48},{48,16},{24,56},{56,24},{64,96... | collective-permute-start | bytes 14155784 | tf_op jit(solution)/shard_map/ppermute | solution.py:20
  398.8 2.2 copy-start.1
  402.6 49.9 %collective-permute-start.3 = (f32[2,6,1,64,6,1,128]{6,3,5,4,2,1,0:T(8,128)}, f32[2,6,1,64,6,1,128]{6,3,5,4,2,1,0:T(8,128)S(1)}, u32[]{:S(2)}, u32[]{:S(2)}) collective-permute-start(f32[2,6,1,64,6,1,128]{6,3,5,4,2,1,0:T(8,128)} %dynamic-slice_bitcast_fusion.2), channel_id=1, source_target_pairs={{0,2},{2,0},{1,3},{3,1},{4,6},{6,4},{5,7},{7,5},{8,10},{10,8},{9,1... | collective-permute-start | bytes 7077896 | tf_op jit(solution)/shard_map/ppermute | solution.py:20
  454.6 18.5 %slice-start.4 = ((s8[6291456]{0:T(1024)(128)(4,1)}), s8[4194304]{0:T(1024)(128)(4,1)S(1)}, s32[]{:S(2)}) async-start(s8[6291456]{0:T(1024)(128)(4,1)} %bitcast.132), calls=%async_computation.4 | async-start | bytes 8388608
  461.2 11.9 %slice-start.5 = ((s8[6291456]{0:T(1024)(128)(4,1)}), s8[2097152]{0:T(1024)(128)(4,1)S(1)}, s32[]{:S(2)}) async-start(s8[6291456]{0:T(1024)(128)(4,1)} %bitcast.132), calls=%async_computation.5 | async-start | bytes 4194304
  505.3 101.1 %collective-permute-start.4 = (f32[2,6,1,64,2,6,1,128]{7,3,6,5,4,2,1,0:T(8,128)}, f32[2,6,1,64,2,6,1,128]{7,3,6,5,4,2,1,0:T(8,128)}, u32[]{:S(2)}, u32[]{:S(2)}) collective-permute-start(f32[2,6,1,64,2,6,1,128]{7,3,6,5,4,2,1,0:T(8,128)} %bitcast.125), channel_id=1, source_target_pairs={{0,16},{16,0},{8,24},{24,8},{32,48},{48,32},{40,56},{56,40},{64,80... | collective-permute-start | bytes 14155784 | tf_op jit(solution)/shard_map/ppermute | solution.py:20
  612.4 2.2 copy-start.2
  616.2 17.4 %collective-permute-start.5 = (f32[2,6,1,64,6,1,128]{6,3,5,4,2,1,0:T(8,128)}, f32[2,6,1,64,6,1,128]{6,3,5,4,2,1,0:T(8,128)S(1)}, u32[]{:S(2)}, u32[]{:S(2)}) collective-permute-start(f32[2,6,1,64,6,1,128]{6,3,5,4,2,1,0:T(8,128)} %dynamic-slice_bitcast_fusion.1), channel_id=1, source_target_pairs={{0,1},{1,0},{2,3},{3,2},{4,5},{5,4},{6,7},{7,6},{8,9},{9,8},{10,11... | collective-permute-start | bytes 7077896 | tf_op jit(solution)/shard_map/ppermute | solution.py:20
  635.7 18.5 %slice-start = ((s8[6291456]{0:T(1024)(128)(4,1)}), s8[4194304]{0:T(1024)(128)(4,1)S(1)}, s32[]{:S(2)}) async-start(s8[6291456]{0:T(1024)(128)(4,1)} %bitcast.128), calls=%async_computation | async-start | bytes 8388608
  642.4 11.9 %slice-start.1 = ((s8[6291456]{0:T(1024)(128)(4,1)}), s8[2097152]{0:T(1024)(128)(4,1)S(1)}, s32[]{:S(2)}) async-start(s8[6291456]{0:T(1024)(128)(4,1)} %bitcast.128), calls=%async_computation.1 | async-start | bytes 4194304
  752.2 103.8 %collective-permute-start.6 = (f32[2,6,1,64,6,1,2,64]{7,3,4,6,1,0,5,2:T(8,128)}, f32[2,6,1,64,6,1,2,64]{7,3,4,6,1,0,5,2:T(8,128)}, u32[]{:S(2)}, u32[]{:S(2)}) collective-permute-start(f32[2,6,1,64,6,1,2,64]{7,3,4,6,1,0,5,2:T(8,128)} %dynamic-slice_bitcast_fusion), channel_id=1, source_target_pairs={{0,8},{8,0},{16,24},{24,16},{32,40},{40,32},{48,56},{56,48},{64,72... | collective-permute-start | bytes 7077896 | tf_op jit(solution)/shard_map/ppermute | solution.py:20
where the time goes:
time: 877 us; the launch traced here: 873 us
  waiting for transfers between devices  478 us (55%)
  other arithmetic  182 us (21%)
  local copies, waits for them, and re-layouts  99.1 us (11%)
  matrix products  95.9 us (11%)
  starting transfers between devices  18 us (2%)
    ppermute x7, waiting for transfers between devices, partner(): return lax.ppermute(block, axis, route)  478 us
    add x3, other arithmetic, shards(): imag_part = cosine * interp[1] + sine_part * interp[0]  79.4 us
    dot_general x4, matrix products, shards(): jnp.einsum('puv,zqtavb->zqtapub', lagrange, interp, precision=highest)  48 us
    reduce_sum x1, other arithmetic, shards(): terms = jnp.einsum('zabcdefghij->z' + spec_x + spec_y, terms)  36.1 us
    reshape x4, local copies, waits for them, and re-layouts, shards(): speed_vals.reshape(2, order_count, local_x, 2, order_count, local_y)  29 us
    dot_general x4, matrix products, shards(): jnp.einsum('qts,zsaub->zqtaub', lagrange, current, precision=highest)  27.2 us
    sub x1, other arithmetic, shards(): real_part = cosine * interp[0] - sine_part * interp[1]  26.2 us
    add x4, other arithmetic, trade_x(): return kept_half + partner(sent_half, 'bx', dev_bits - 1 - level_index)  22.9 us
  transfers between devices with their start and end apart: 7, of which 6 were waited for; matrix products, arithmetic and copies ran while one was open for 4% of the time, Pallas kernels for 0%

commit v1 on v0

v1 whole, which is shorter than its diff:
```python
import functools

import jax
import jax.numpy as jnp
import ml_dtypes
import numpy as np
from jax import lax
from jax.experimental import pallas as pl
from jax.experimental.pallas import tpu as pltpu
from jax.sharding import PartitionSpec as P

N = 2048
CHEB = 6
HALF = CHEB * CHEB
ROWS = 2 * HALF
TERMS = 4 * HALF
PAD = 80
LANES = 128
MESH = pl.DeviceIdType.MESH


def cheb_points():
    return np.cos(np.pi * (2 * np.arange(CHEB) + 1) / (2 * CHEB))


def lagrange_table():
    points = cheb_points()
    weights = np.zeros((2, CHEB, CHEB))
    for quadrant in range(2):
        shifted = quadrant - 0.5 + points / 2
        for target in range(CHEB):
            for source in range(CHEB):
                product = 1.0
                for other in range(CHEB):
                    if other != source:
                        product = (
                            product
                            * (shifted[target] - points[other])
                            / (points[source] - points[other])
                        )
                weights[quadrant, target, source] = product
    return weights


def turns_table():
    return np.arange(2)[:, None] + (1.0 + cheb_points())[None, :] / 2.0


def split16(values):
    high = values.astype(ml_dtypes.bfloat16)
    low = (values - high.astype(np.float64)).astype(ml_dtypes.bfloat16)
    return high, low


def mixing_tables():
    weights = lagrange_table()
    turns = turns_table()
    tables = []
    for c1, c2 in ((0, 0), (0, 1), (1, 0), (1, 1), (0, None), (1, None)):
        phase1 = np.exp(2j * np.pi * (c1 - 0.5) * turns)
        phase2 = np.exp(2j * np.pi * (0 if c2 is None else c2 - 0.5) * turns)
        w1 = weights * phase1[:, :, None]
        w2 = weights * phase2[:, :, None]
        full = np.einsum("qts,puv->qptusv", w1, w2).reshape(TERMS, HALF)
        real = np.block([[full.real, -full.imag], [full.imag, full.real]])
        high, low = split16(real)
        table = np.zeros((2 * TERMS, 3 * PAD), ml_dtypes.bfloat16)
        table[:, 0:ROWS] = high
        table[:, PAD : PAD + ROWS] = high
        table[:, 2 * PAD : 2 * PAD + ROWS] = low
        tables.append(table)
    return np.stack(tables)


def row_tables():
    q1, q2, t1, t2 = [
        axis.reshape(-1) for axis in np.meshgrid(*[np.arange(n) for n in (2, 2, CHEB, CHEB)], indexing="ij")
    ]
    rows = np.stack([CHEB * q1 + t1, CHEB * q2 + t2, turns_table()[q2, t2]])
    return np.broadcast_to(rows[:, :, None], (3, TERMS, LANES)).astype(np.float32)


def fit(function, degree):
    count = 200
    s = 0.125 * (1 + np.cos(np.pi * (2 * np.arange(count) + 1) / (2 * count)))
    series = np.polynomial.chebyshev.Chebyshev.fit(s, function(np.sqrt(s)), degree, domain=[0, 0.25])
    return [float(c) for c in series.convert(kind=np.polynomial.Polynomial).coef]


SIN = fit(lambda r: np.sin(2 * np.pi * r) / r, 5)
COS = fit(lambda r: np.cos(2 * np.pi * r), 5)


def horner(coefficients, s):
    value = s * coefficients[-1] + coefficients[-2]
    for coefficient in coefficients[-3::-1]:
        value = value * s + coefficient
    return value


def unit(turns):
    r = turns - jnp.round(turns)
    s = r * r
    return horner(COS, s), horner(SIN, s) * r


def operand(block):
    block = jnp.concatenate([block, jnp.zeros((PAD - ROWS, block.shape[1]), jnp.float32)], axis=0)
    high = block.astype(jnp.bfloat16)
    low = (block - high.astype(jnp.float32)).astype(jnp.bfloat16)
    return jnp.concatenate([high, low, high], axis=0)


def reverse6(value):
    total = 0
    for bit in range(6):
        total = total + lax.rem(lax.div(value, 1 << bit), 2) * (1 << (5 - bit))
    return total


def kernel(
    coef_ref, slow_ref, mix_ref, rows_ref, out_ref,
    sbuf, xin, s0, z1, zr, s2, obuf, orecv, vtab, lane_ref, m_ref, y_ref, acc_ref,
    in_send, in_recv, sib_send, sib_recv, out_send, out_recv,
):
    bx, by = lax.axis_index("bx"), lax.axis_index("by")
    my_z, my_x = lax.div(bx, 4), lax.rem(bx, 4)
    my_y, core = lax.div(by, 2), lax.rem(by, 2)
    chip = bx * 4 + my_y
    low1 = reverse6(chip) * 16

    for ell in range(64):
        for tile in range(9):
            sbuf[ell, 8 * tile : 8 * tile + 8, :] = coef_ref[pl.ds(tile * 512 + ell, 8, stride=64), :]

    local_in = pltpu.make_async_copy(sbuf.at[chip], xin.at[0, my_z, my_y], in_recv.at[0])
    local_in.start()

    def send_in(step, carry):
        hop_x = lax.div(step, 16)
        dx = hop_x + lax.div(hop_x, 2) * (1 - 2 * lax.rem(hop_x, 2))
        dz, dy = lax.div(lax.rem(step, 16), 4), lax.rem(step, 4)
        to_x, to_z, to_y = lax.rem(my_x + dx, 4), lax.rem(my_z + dz, 4), lax.rem(my_y + dy, 4)
        pltpu.make_async_remote_copy(
            src_ref=sbuf.at[to_z * 16 + to_x * 4 + to_y],
            dst_ref=xin.at[dx, my_z, my_y],
            send_sem=in_send,
            recv_sem=in_recv.at[dx],
            device_id=(to_z * 4 + to_x, to_y * 2 + core),
            device_id_type=MESH,
        ).start()
        return carry

    lax.fori_loop(1, 64, send_in, 0)

    lane = lax.broadcasted_iota(jnp.int32, (TERMS, 96), 1).astype(jnp.float32)
    row_i = rows_ref[0, :, 0:96]
    row_j = rows_ref[1, :, 0:96]

    def spread(level, a1):
        pick = jnp.where(row_i + (12 * a1).astype(jnp.float32) == lane, 1.0, 0.0)
        return jnp.dot(pick, slow_ref[level], precision=lax.Precision.HIGHEST, preferred_element_type=jnp.float32)

    def place(slot, spreaded, a2):
        picked = jnp.where(row_j + (12 * a2).astype(jnp.float32) == lane, spreaded, 0.0)
        column = jnp.sum(picked, axis=1, keepdims=True)
        vtab[slot] = jnp.broadcast_to(column, (TERMS, LANES))

    zero = jnp.int32(0)
    place(0, spread(0, zero), zero)

    def fill1(a1, carry):
        table = spread(1, a1)
        for a2 in range(2):
            place(1 + 2 * a1 + a2, table, jnp.int32(a2))
        return carry

    lax.fori_loop(0, 2, fill1, 0)

    def fill2(z, carry):
        table = spread(2, z)
        for y1 in range(2):
            place(5 + 2 * z + y1, table, 2 * y1 + core)
        return carry

    lax.fori_loop(0, 4, fill2, 0)

    def fill3(a1, carry):
        table = spread(3, a1)
        for y1 in range(2):
            for c in range(2):
                place(13 + 4 * a1 + 2 * y1 + c, table, 2 * (2 * y1 + core) + c)
        return carry

    lax.fori_loop(0, 8, fill3, 0)

    lanes = lax.broadcasted_iota(jnp.int32, (8, LANES), 1)
    bit3 = lanes // 64
    lane_ref[...] = bit3 * 8 + reverse6(lanes % 64) * 16

    def magnitude(level, r1, c1, r2, c2):
        width = 2.0 ** (level + 1)
        k = (lax.div(r1, 1 << level).astype(jnp.float32) + 0.5) * width - N / 2
        step = (c1.astype(jnp.float32) - 0.5) * width
        k0 = k - step
        k2 = (lax.shift_right_logical(r2, jnp.full(r2.shape, level, jnp.int32)).astype(jnp.float32) + 0.5) * width - N / 2
        step2 = (c2.astype(jnp.float32) - 0.5) * width
        k20 = k2 - step2
        above = step * (k + k0) + step2 * (k2 + k20)
        return above / (jnp.sqrt(k * k + k2 * k2) + jnp.sqrt(k0 * k0 + k20 * k20))

    def combine(count, slots, shift):
        def tile(i, carry):
            at = pl.ds(pl.multiple_of(8 * i, 8), 8)
            at_im = pl.ds(pl.multiple_of(8 * i + TERMS, 8), 8)
            for side in range(2):
                cols = pl.ds(side * LANES, LANES)
                v = vtab[slots[side], at, :]
                total_re = total_im = None
                for c in range(count):
                    turns = v * m_ref[c, side]
                    if shift is not None:
                        turns = turns + rows_ref[2, at, :] * shift
                    co, si = unit(turns)
                    y_re, y_im = y_ref[c, at, cols], y_ref[c, at_im, cols]
                    re = co * y_re - si * y_im
                    im = co * y_im + si * y_re
                    total_re = re if total_re is None else total_re + re
                    total_im = im if total_im is None else total_im + im
                acc_ref[at, cols] = total_re
                acc_ref[at_im, cols] = total_im
            return carry

        lax.fori_loop(0, TERMS // 8, tile, 0)

    def fold(side, q1, q2, put):
        cols = pl.ds(side * LANES, LANES)
        base = q1 * ROWS + q2 * HALF
        put(pl.ds(0, HALF), acc_ref[base : base + HALF, cols])
        put(pl.ds(HALF, HALF), acc_ref[TERMS + base : TERMS + base + HALF, cols])

    one = jnp.int32(1)

    def chunk(step, carry):
        dx = step + lax.div(step, 2) * (1 - 2 * lax.rem(step, 2))
        x = lax.rem(my_x - dx + 4, 4)
        x1, x0 = lax.div(x, 2), lax.rem(x, 2)
        high1 = low1 + 4 * x1 + 8 * x0
        pltpu.make_async_copy(xin.at[dx], xin.at[dx], in_recv.at[dx]).wait()

        def level0(z0, carry):
            for c1 in range(2):
                for c2 in range(2):
                    child = 2 * c1 + c2
                    blocks = []
                    for y0 in range(2):
                        blocks.append(xin[dx, 2 * c1 + z0, 2 * c2 + y0])
                        r1 = high1 + c1 + 2 * z0
                        r2 = lane_ref[...] + (c2 + 2 * y0 + 4 * core)
                        m_ref[child, y0] = magnitude(0, r1, c1 * one, r2, c2 * one)
                    y_ref[child] = jnp.dot(
                        mix_ref[child], operand(jnp.concatenate(blocks, axis=1)), preferred_element_type=jnp.float32
                    )
            combine(4, (0, 0), None)
            for y0 in range(2):
                for q1 in range(2):
                    for q2 in range(2):

                        def put(rows, values, q1=q1, q2=q2, y0=y0):
                            s0[2 * q1 + z0, 2 * q2 + y0, rows, :] = values

                        fold(y0, q1, q2, put)
            return carry

        lax.fori_loop(0, 2, level0, 0)

        def level1(a1, carry):
            for c1 in range(2):
                for c2 in range(2):
                    child = 2 * c1 + c2
                    blocks = []
                    for a2 in range(2):
                        blocks.append(s0[2 * a1 + c1, 2 * a2 + c2])
                        r1 = high1 + 2 * c1
                        r2 = lane_ref[...] + (2 * c2 + 4 * core)
                        m_ref[child, a2] = magnitude(1, r1, c1 * one, r2, c2 * one)
                    y_ref[child] = jnp.dot(
                        mix_ref[child], operand(jnp.concatenate(blocks, axis=1)), preferred_element_type=jnp.float32
                    )
            combine(4, (1 + 2 * a1, 2 + 2 * a1), None)
            for a2 in range(2):
                for q1 in range(2):
                    for q2 in range(2):

                        def put(rows, values, q1=q1, q2=q2, a2=a2):
                            z1[x, q2, 2 * a1 + q1, a2, rows, :] = values

                        fold(a2, q1, q2, put)
            return carry

        lax.fori_loop(0, 2, level1, 0)
        pltpu.make_async_remote_copy(
            src_ref=z1.at[x, 1 - core],
            dst_ref=zr.at[x],
            send_sem=sib_send.at[dx],
            recv_sem=sib_recv.at[dx],
            device_id=(bx, my_y * 2 + 1 - core),
            device_id_type=MESH,
        ).start()
        return carry

    lax.fori_loop(0, 4, chunk, 0)

    def sibling(dx, carry):
        pltpu.make_async_copy(zr.at[0], zr.at[0], sib_recv.at[dx]).wait()
        pltpu.make_async_copy(zr.at[0], zr.at[0], sib_send.at[dx]).wait()
        return carry

    lax.fori_loop(0, 4, sibling, 0)

    def target(step, carry):
        z = lax.rem(my_z + lax.div(step, 2) + 2, 4)
        y1 = lax.rem(lax.div(my_y, 2) + lax.rem(step, 2), 2)
        y = 2 * y1 + core
        for c1 in range(2):
            for other in range(2):
                child = 2 * c1 + other
                c2 = core + other * (1 - 2 * core)
                blocks = []
                for x0 in range(2):
                    x = 2 * c1 + x0
                    blocks.append(zr[x, z, y1] if other else z1[x, core, z, y1])
                    r1 = low1 + 4 * c1 + 8 * x0
                    r2 = lane_ref[...] + 4 * c2
                    m_ref[child, x0] = magnitude(2, r1, c1 * one, r2, c2)
                y_ref[child] = jnp.dot(
                    mix_ref[2 * c1 + c2], operand(jnp.concatenate(blocks, axis=1)), preferred_element_type=jnp.float32
                )
        slot = 5 + 2 * z + y1
        combine(4, (slot, slot), None)
        for x0 in range(2):
            for q1 in range(2):
                for q2 in range(2):

                    def put(rows, values, q1=q1, q2=q2, x0=x0):
                        s2[q1, q2, x0, rows, :] = values

                    fold(x0, q1, q2, put)

        def level3(x1, carry):
            for c1 in range(2):
                blocks = []
                for c in range(2):
                    blocks.append(s2[x1, c, c1])
                    r1 = low1 + 8 * c1
                    m_ref[c1, c] = magnitude(3, r1, c1 * one, lane_ref[...], bit3)
                y_ref[c1] = jnp.dot(
                    mix_ref[4 + c1], operand(jnp.concatenate(blocks, axis=1)), preferred_element_type=jnp.float32
                )
            slot = 13 + 4 * (2 * z + x1) + 2 * y1
            combine(2, (slot, slot + 1), bit3.astype(jnp.float32) - 0.5)
            left = lax.broadcasted_iota(jnp.int32, (HALF, LANES), 1) < 64
            for c in range(2):
                cols = pl.ds(c * LANES, LANES)
                for q1 in range(2):
                    for part in range(2):
                        base = part * TERMS + q1 * ROWS
                        first = acc_ref[base : base + HALF, cols]
                        second = acc_ref[base + HALF : base + ROWS, cols]
                        kept = jnp.where(left, first, second)
                        moved = jnp.where(left, second, first)
                        obuf[2 * step + x1, q1, c, HALF * part : HALF * part + HALF, :] = kept + pltpu.roll(moved, 64, 1)
            for q1 in range(2):
                for c in range(2):
                    to_bx = z * 4 + 2 * x1 + q1
                    to_by = 2 * y + c
                    src = obuf.at[2 * step + x1, q1, c]
                    dst = orecv.at[chip]
                    here = jnp.logical_and(to_bx == bx, to_by == by)

                    @pl.when(here)
                    def _(src=src, dst=dst):
                        pltpu.make_async_copy(src, dst, out_recv).start()

                    @pl.when(jnp.logical_not(here))
                    def _(src=src, dst=dst, to_bx=to_bx, to_by=to_by):
                        pltpu.make_async_remote_copy(
                            src_ref=src, dst_ref=dst, send_sem=out_send, recv_sem=out_recv,
                            device_id=(to_bx, to_by), device_id_type=MESH,
                        ).start()

            return carry

        lax.fori_loop(0, 2, level3, 0)
        return carry

    lax.fori_loop(0, 8, target, 0)

    pltpu.make_async_copy(sbuf.at[pl.ds(0, 63)], sbuf.at[pl.ds(0, 63)], in_send).wait()
    kept_here = lax.rem(my_y, 2) == core

    @pl.when(kept_here)
    def _():
        pltpu.make_async_copy(orecv.at[pl.ds(0, 63)], orecv.at[pl.ds(0, 63)], out_send).wait()

    @pl.when(jnp.logical_not(kept_here))
    def _():
        pltpu.make_async_copy(orecv, orecv, out_send).wait()

    pltpu.make_async_copy(orecv, orecv, out_recv).wait()
    for ell in range(64):
        for tile in range(9):
            out_ref[pl.ds(tile * 512 + ell, 8, stride=64), :] = orecv[ell, 8 * tile : 8 * tile + 8, :]


def shards(coefficients, slowness):
    rows = jnp.transpose(coefficients, (0, 1, 3, 2, 4)).reshape(ROWS * 64, LANES)
    block = (ROWS, LANES)
    scratch = [
        pltpu.VMEM((64,) + block, jnp.float32),
        pltpu.VMEM((4, 4, 4) + block, jnp.float32),
        pltpu.VMEM((4, 4) + block, jnp.float32),
        pltpu.VMEM((4, 2, 4, 2) + block, jnp.float32),
        pltpu.VMEM((4, 4, 2) + block, jnp.float32),
        pltpu.VMEM((2, 2, 2) + block, jnp.float32),
        pltpu.VMEM((16, 2, 2) + block, jnp.float32),
        pltpu.VMEM((64,) + block, jnp.float32),
        pltpu.VMEM((45, TERMS, LANES), jnp.float32),
        pltpu.VMEM((8, LANES), jnp.int32),
        pltpu.VMEM((4, 2, 8, LANES), jnp.float32),
        pltpu.VMEM((4, 2 * TERMS, 2 * LANES), jnp.float32),
        pltpu.VMEM((2 * TERMS, 2 * LANES), jnp.float32),
        pltpu.SemaphoreType.DMA,
        pltpu.SemaphoreType.DMA((4,)),
        pltpu.SemaphoreType.DMA((4,)),
        pltpu.SemaphoreType.DMA((4,)),
        pltpu.SemaphoreType.DMA,
        pltpu.SemaphoreType.DMA,
    ]
    vmem = pl.BlockSpec(memory_space=pltpu.VMEM)
    out = pl.pallas_call(
        kernel,
        out_shape=jax.ShapeDtypeStruct((ROWS * 64, LANES), jnp.float32),
        in_specs=[vmem] * 4,
        out_specs=vmem,
        scratch_shapes=scratch,
        compiler_params=pltpu.CompilerParams(has_side_effects=True, vmem_limit_bytes=50 << 20),
    )(rows, slowness, jnp.asarray(mixing_tables()), jnp.asarray(row_tables()))
    return jnp.transpose(out.reshape(2, CHEB, CHEB, 64, LANES), (0, 1, 3, 2, 4))


def solution(mesh):
    placed = (P(None, None, "bx", None, "by"), P())
    return jax.shard_map(
        shards,
        mesh=mesh,
        in_specs=placed,
        out_specs=P(None, None, "bx", None, "by"),
        check_vma=False,
    )
```

time: 877 us -> 115 us (0.13)
  waiting for transfers between devices: 478 us -> 0 us
  other arithmetic: 182 us -> 0 us
  Pallas kernels: 0 us -> 110 us
  matrix products: 95.9 us -> 0 us
  local copies, waits for them, and re-layouts: 99.1 us -> 4.44 us
  starting transfers between devices: 18 us -> 0 us
    ppermute x7 -> x0, waiting for transfers between devices: 478 us -> none  [partner(): return lax.ppermute(block, axis, route)]
    pallas_call x0 -> x1, Pallas kernels: none -> 110 us  [shards(): pl.pallas_call(kernel, out_shape=jax.ShapeDtypeStruct((ROWS * 64, LANES),...]
    add x15 -> x0, other arithmetic: 102 us -> none  [the longest x3 79.4 us: shards(): imag_part = cosine * interp[1] + sine_part * interp[0]]
    dot_general x16 -> x0, matrix products: 95.9 us -> none  [the longest x4 48 us: shards(): jnp.einsum('puv,zqtavb->zqtapub', lagrange, interp, precision=highest)]
    reduce_sum x1 -> x0, other arithmetic: 36.1 us -> none  [shards(): terms = jnp.einsum('zabcdefghij->z' + spec_x + spec_y, terms)]
    reshape x5 -> x0, local copies, waits for them, and re-layouts: 34.6 us -> none  [the longest x4 29 us: shards(): speed_vals.reshape(2, order_count, local_x, 2, order_count, local_y)]
    sub x5 -> x0, other arithmetic: 26.6 us -> none  [the longest x1 26.2 us: shards(): real_part = cosine * interp[0] - sine_part * interp[1]]
    another operation x2 -> x0, local copies, waits for them, and re-layouts: 20.5 us -> none  [shards(): terms = jnp.stack([real_part, imag_part])]
  transfers between devices with their start and end apart: 7 -> 0, of which waited for: 6 -> 0; matrix products, arithmetic and copies ran while one was open for 4% -> 0% of each run, Pallas kernels for 0% -> 0%
where the time goes in v1:
time: 115 us; the launch traced here: 114 us
  Pallas kernels  110 us (96%)
  local copies, waits for them, and re-layouts  4.44 us (4%)
    pallas_call x1, Pallas kernels, shards(): pl.pallas_call(kernel, out_shape=jax.ShapeDtypeStruct((ROWS * 64, LANES),...  110 us
    unnamed x7, local copies, waits for them, and re-layouts  4.44 us

profile of v1, /device:TPU:1, one launch (start us, length us, event | category | flops | bytes accessed | tf_op | source)
XLA Modules:
  0.0 114.3 jit_solution(9768921113654789852)
XLA Ops:
  0.0 0.0 copy-start
  0.0 1.2 %copy-done = bf16[6,288,240]{2,1,0:T(8,128)(2,1)S(1)} copy-done((bf16[6,288,240]{2,1,0:T(8,128)(2,1)S(1)}, bf16[6,288,240]{2,1,0:T(8,128)(2,1)}, u32[]{:S(2)}) %copy-start) | copy-done | bytes 829464
  1.2 0.0 copy-start.1
  1.2 0.9 copy-done.1
  2.1 0.0 copy-start.2
  2.1 0.9 copy-done.2
  3.0 109.9 %shard_map.46 = f32[4608,128]{1,0:T(8,128)S(1)} custom-call(f32[4608,128]{1,0:T(8,128)} %bitcast.7, f32[4,96,96]{2,1,0:T(8,128)S(1)} %copy-done.2, bf16[6,288,240]{2,1,0:T(8,128)(2,1)S(1)} %copy-done, f32[3,144,128]{2,1,0:T(8,128)S(1)} %copy-done.1), custom_call_target="tpu_custom_call" | custom-call | tf_op jit(solution)/shard_map/pallas_call | solution.py:441
  112.9 1.4 %copy.6 = f32[2,6,64,6,128]{4,2,3,1,0:T(8,128)} copy(f32[2,6,64,6,128]{4,2,3,1,0:T(8,128)S(1)} %bitcast.6) | data formatting | bytes 4718592
Async XLA Ops:
  0.0 1.2 %copy-start = (bf16[6,288,240]{2,1,0:T(8,128)(2,1)S(1)}, bf16[6,288,240]{2,1,0:T(8,128)(2,1)}, u32[]{:S(2)}) copy-start(bf16[6,288,240]{2,1,0:T(8,128)(2,1)} %constant.4.clone.mix_ref) | copy-start | bytes 2488324
  1.2 0.9 copy-start.1
  2.1 0.9 copy-start.2

commit v2 on v1

v2 whole, which is shorter than its diff:
```python
import functools

import jax
import jax.numpy as jnp
import ml_dtypes
import numpy as np
from jax import lax
from jax.experimental import pallas as pl
from jax.experimental.pallas import tpu as pltpu
from jax.sharding import PartitionSpec as P

N = 2048
CHEB = 6
HALF = CHEB * CHEB
ROWS = 2 * HALF
TERMS = 4 * HALF
PAD = 80
LANES = 128
MESH = pl.DeviceIdType.MESH


def cheb_points():
    return np.cos(np.pi * (2 * np.arange(CHEB) + 1) / (2 * CHEB))


def lagrange_table():
    points = cheb_points()
    weights = np.zeros((2, CHEB, CHEB))
    for quadrant in range(2):
        shifted = quadrant - 0.5 + points / 2
        for target in range(CHEB):
            for source in range(CHEB):
                product = 1.0
                for other in range(CHEB):
                    if other != source:
                        product = (
                            product
                            * (shifted[target] - points[other])
                            / (points[source] - points[other])
                        )
                weights[quadrant, target, source] = product
    return weights


def turns_table():
    return np.arange(2)[:, None] + (1.0 + cheb_points())[None, :] / 2.0


def split16(values):
    high = values.astype(ml_dtypes.bfloat16)
    low = (values - high.astype(np.float64)).astype(ml_dtypes.bfloat16)
    return high, low


def mixing_tables():
    weights = lagrange_table()
    turns = turns_table()
    tables = []
    for parts in ((0, HALF), (0, 40), (4, 44)):
        for c1, c2 in ((0, 0), (0, 1), (1, 0), (1, 1)):
            w1 = weights * np.exp(2j * np.pi * (c1 - 0.5) * turns)[:, :, None]
            w2 = weights * np.exp(2j * np.pi * (c2 - 0.5) * turns)[:, :, None]
            full = np.einsum("qts,puv->qptusv", w1, w2).reshape(TERMS, HALF)
            real = np.zeros((2 * TERMS, PAD))
            real[:, parts[0] : parts[0] + HALF] = np.concatenate([full.real, full.imag])
            real[:, parts[1] : parts[1] + HALF] = np.concatenate([-full.imag, full.real])
            high, low = split16(real)
            tables.append(np.concatenate([high, high, low], axis=1))
    return np.stack(tables)


def row_tables():
    q1, q2, t1, t2 = [
        axis.reshape(-1) for axis in np.meshgrid(*[np.arange(n) for n in (2, 2, CHEB, CHEB)], indexing="ij")
    ]
    rows = np.stack([CHEB * q1 + t1, CHEB * q2 + t2])
    return np.broadcast_to(rows[:, :, None], (2, TERMS, LANES)).astype(np.float32)


def fit(function, degree):
    count = 200
    s = 0.125 * (1 + np.cos(np.pi * (2 * np.arange(count) + 1) / (2 * count)))
    series = np.polynomial.chebyshev.Chebyshev.fit(s, function(np.sqrt(s)), degree, domain=[0, 0.25])
    return [float(c) for c in series.convert(kind=np.polynomial.Polynomial).coef]


SIN = fit(lambda r: np.sin(2 * np.pi * r) / r, 5)
COS = fit(lambda r: np.cos(2 * np.pi * r), 5)


def horner(coefficients, s):
    value = s * coefficients[-1] + coefficients[-2]
    for coefficient in coefficients[-3::-1]:
        value = value * s + coefficient
    return value


def unit(turns):
    r = turns - jnp.round(turns)
    s = r * r
    return horner(COS, s), horner(SIN, s) * r


def operand(block):
    if block.shape[0] < PAD:
        block = jnp.concatenate([block, jnp.zeros((PAD - block.shape[0], block.shape[1]), jnp.float32)], axis=0)
    high = block.astype(jnp.bfloat16)
    low = (block - high.astype(jnp.float32)).astype(jnp.bfloat16)
    return jnp.concatenate([high, low, high], axis=0)


def reverse6(value):
    total = 0
    for bit in range(6):
        total = total + lax.rem(lax.div(value, 1 << bit), 2) * (1 << (5 - bit))
    return total


def kernel(
    coef_hbm, slow_hbm, mix_hbm, rows_hbm, out_ref,
    coef_ref, slow_ref, mix_ref, rows_ref,
    sbuf, xin, s0, z1, zr, s2, obuf, orecv, vtab, e_tab, y_a, y_b, acc_a, acc_b,
    load, in_send, in_recv, sib_send, sib_recv, out_send, out_recv,
):
    bx, by = lax.axis_index("bx"), lax.axis_index("by")
    my_z, my_x = lax.div(bx, 4), lax.rem(bx, 4)
    my_y, core = lax.div(by, 2), lax.rem(by, 2)
    my_x0 = lax.rem(my_x, 2)
    chip = bx * 4 + my_y
    low1 = reverse6(chip) * 16

    loads = [
        pltpu.make_async_copy(src, dst, load.at[i])
        for i, (src, dst) in enumerate(
            ((coef_hbm, coef_ref), (slow_hbm, slow_ref), (rows_hbm, rows_ref), (mix_hbm, mix_ref))
        )
    ]
    for copy in loads:
        copy.start()
    loads[0].wait()

    def send_in(step, carry):
        part, inner = lax.div(step, 16), lax.rem(step, 16)
        pz, py = lax.div(part, 2), lax.rem(lax.rem(part, 2) + core, 2)
        other = lax.div(inner, 4)
        dx = lax.rem(lax.rem(inner, 4) + other, 4)
        dz, dy = 2 * lax.div(other, 2) + pz, 2 * lax.rem(other, 2) + py
        sign = 1 - 2 * core
        dx, dz, dy = [lax.rem(4 + sign * d, 4) for d in (dx, dz, dy)]
        to_x, to_z, to_y = lax.rem(my_x + dx, 4), lax.rem(my_z + dz, 4), lax.rem(my_y + dy, 4)
        to_bx, to_by = to_z * 4 + to_x, to_y * 2 + my_x0
        ell = to_z * 16 + to_x * 4 + to_y
        for tile in range(9):
            sbuf[ell, 8 * tile : 8 * tile + 8, :] = coef_ref[pl.ds(tile * 512 + ell, 8, stride=64), :]
        src = sbuf.at[ell]
        dst = xin.at[lax.div(dx, 2), core, my_z, my_y]
        here = jnp.logical_and(to_bx == bx, to_by == by)

        @pl.when(here)
        def _():
            pltpu.make_async_copy(src, dst, in_recv.at[part]).start()

        @pl.when(jnp.logical_not(here))
        def _():
            pltpu.make_async_remote_copy(
                src_ref=src, dst_ref=dst, send_sem=in_send, recv_sem=in_recv.at[part],
                device_id=(to_bx, to_by), device_id_type=MESH,
            ).start()

        return carry

    lax.fori_loop(0, 64, send_in, 0)

    loads[1].wait()
    loads[2].wait()
    lane = lax.broadcasted_iota(jnp.int32, (TERMS, 96), 1).astype(jnp.float32)
    row_i = rows_ref[0, :, 0:96]
    row_j = rows_ref[1, :, 0:96]

    def spread(level, a1):
        pick = jnp.where(row_i + (12 * a1).astype(jnp.float32) == lane, 1.0, 0.0)
        return jnp.dot(pick, slow_ref[level], precision=lax.Precision.HIGHEST, preferred_element_type=jnp.float32)

    def column(table, a2):
        picked = jnp.where(row_j + (12 * a2).astype(jnp.float32) == lane, table, 0.0)
        return jnp.broadcast_to(jnp.sum(picked, axis=1, keepdims=True), (TERMS, LANES))

    zero, one = jnp.int32(0), jnp.int32(1)
    vtab[0] = column(spread(0, zero), zero)

    def fill1(a1, carry):
        table = spread(1, a1)
        for a2 in range(2):
            vtab[1 + 2 * a1 + a2] = column(table, a2 * one)
        return carry

    lax.fori_loop(0, 2, fill1, 0)

    def fill2(z, carry):
        table = spread(2, z)
        for a2 in range(2):
            vtab[5 + 2 * z + a2] = column(table, 2 * a2 + core)
        return carry

    lax.fori_loop(0, 4, fill2, 0)
    left_rows = lax.broadcasted_iota(jnp.int32, (TERMS, LANES), 1) < 64

    def fill3(a1, carry):
        table = spread(3, a1)
        for a2 in range(2):
            box = 2 * (2 * a2 + core)
            vtab[13 + 2 * a1 + a2] = jnp.where(left_rows, column(table, box), column(table, box + 1))
        return carry

    lax.fori_loop(0, 8, fill3, 0)

    lanes = lax.broadcasted_iota(jnp.int32, (8, LANES), 1)
    low2 = reverse6(lax.rem(lanes, 64)) * 16
    lane2 = lax.div(lanes, 64) * 8 + low2
    back = 127 - lanes
    back_half = lax.div(lanes, 64) * 64 + 63 - lax.rem(lanes, 64)

    def permute(block, index):
        rows = [
            jnp.take_along_axis(block[8 * i : 8 * i + 8], index, axis=1, mode="promise_in_bounds")
            for i in range(block.shape[0] // 8)
        ]
        return jnp.concatenate(rows, axis=0)

    def magnitude(level, r1, c1, r2, c2):
        width = 2.0 ** (level + 1)
        k = (lax.div(r1, 1 << level).astype(jnp.float32) + 0.5) * width - N / 2
        step = (c1 - 0.5) * width
        k0 = k - step
        k2 = (lax.div(r2, jnp.full(r2.shape, 1 << level, jnp.int32)).astype(jnp.float32) + 0.5) * width - N / 2
        step2 = (c2 - 0.5) * width
        k20 = k2 - step2
        above = step * (k + k0) + step2 * (k2 + k20)
        return above / (jnp.sqrt(k * k + k2 * k2) + jnp.sqrt(k0 * k0 + k20 * k20))

    def interpolate(y_ref, child, table, blocks):
        y_ref[child] = jnp.dot(
            mix_ref[table], operand(jnp.concatenate(blocks, axis=1)), preferred_element_type=jnp.float32
        )

    def tiles(body):
        def tile(i, carry):
            body(i, pl.ds(pl.multiple_of(8 * i, 8), 8), pl.ds(pl.multiple_of(8 * i + TERMS, 8), 8))
            return carry

        lax.fori_loop(0, TERMS // 8, tile, 0, unroll=True)

    def added(total, co, si, y_ref, child, at, at_im, side):
        cols = pl.ds(side * LANES, LANES)
        y_re, y_im = y_ref[child, at, cols], y_ref[child, at_im, cols]
        re, im = co * y_re - si * y_im, co * y_im + si * y_re
        return (re, im) if total is None else (total[0] + re, total[1] + im)

    def exponentials(entry, slots, sizes):
        def tile(i, carry):
            at = pl.ds(pl.multiple_of(8 * i, 8), 8)
            for j in range(4):
                co, si = unit(vtab[slots[j], at, :] * sizes[j])
                e_tab[entry, j, 0, at, :] = co
                e_tab[entry, j, 1, at, :] = si
            return carry

        lax.fori_loop(0, TERMS // 8, tile, 0, unroll=3)

    def combine_cores(y_ref, dst, entry):
        def body(i, at, at_im):
            totals = [None, None]
            for c1 in range(2):
                for c2 in range(2):
                    co, si = e_tab[entry, 2 * c1 + c2, 0, at, :], e_tab[entry, 2 * c1 + c2, 1, at, :]
                    totals[0] = added(totals[0], co, si, y_ref, 2 * c1 + c2, at, at_im, 0)
                    totals[1] = added(totals[1], co, si, y_ref, 2 * c1 + 1 - c2, at, at_im, 1)
            for side in range(2):
                put(dst[side], i, totals[side])

        tiles(body)

    def combine_mirrored(y_ref, dst, entry, index):
        def body(i, at, at_im):
            for side in range(2):
                totals = [None, None]
                for c1 in range(2):
                    co, si = e_tab[entry, 2 * c1 + side, 0, at, :], e_tab[entry, 2 * c1 + side, 1, at, :]
                    for c2 in range(2):
                        totals[c2] = added(totals[c2], co, si, y_ref, 2 * c1 + c2, at, at_im, side)
                put(dst[side], i, [totals[0][part] + permute(totals[1][part], index) for part in range(2)])

        tiles(body)

    def put(dst, i, total):
        rows = pl.ds(pl.multiple_of(8 * lax.rem(i, 9), 8), 8)
        for part in range(2):
            dst[2 * part + lax.div(i, 9), rows, :] = total[part]

    def window(src, q1, q2):
        rows = pl.ds(pl.multiple_of(32 * q2, 8), 40)
        return jnp.concatenate([src[q1, rows, :], src[2 + q1, rows, :]], axis=0)

    pairs = ((0, y_a, acc_a), (1, y_b, acc_b))

    def x_of(slot):
        dx = 2 * slot + lax.rem(my_x + core, 2)
        x = lax.rem(my_x - dx + 4, 4)
        return lax.div(x, 2), low1 + 4 * lax.div(x, 2) + 8 * core

    def group_of(part):
        return lax.rem(my_z + lax.div(part, 2), 2), lax.rem(my_y + lax.rem(part, 2), 2)

    def box_of(step):
        return lax.rem(lax.div(my_z, 2) + 1 + lax.div(step, 2), 2), lax.rem(lax.div(my_y, 2) + step, 2)

    children = [(c1, c2) for c1 in range(2) for c2 in range(2)]

    def phases0(part, carry):
        z0, y0 = group_of(part)
        for slot in range(2):
            r1 = x_of(slot)[1] + 2 * z0
            sizes = [magnitude(0, r1 + c1, c1, lane2 + (c2 + 2 * y0), c2) for c1, c2 in children]
            exponentials(2 * part + slot, (0,) * 4, sizes)
        return carry

    def phases1(step, carry):
        a1, a2 = box_of(step)
        for slot in range(2):
            r1 = x_of(slot)[1]
            sizes = [magnitude(1, r1 + 2 * c1, c1, lane2 + 2 * c2, c2) for c1, c2 in children]
            exponentials(8 + 2 * step + slot, (1 + 2 * a1 + a2,) * 4, sizes)
        return carry

    def phases2(step, carry):
        a1, a2 = box_of(step)
        sizes = [
            magnitude(2, low1 + 4 * c1 + 8 * x0, c1, lane2, 0) for c1 in range(2) for x0 in (core, 1 - core)
        ]
        for z0 in range(2):
            exponentials(16 + 2 * step + z0, (5 + 2 * (2 * a1 + z0) + a2,) * 4, sizes)
        return carry

    def phases3(step, carry):
        a1, a2 = box_of(step)
        sizes = [magnitude(3, low1 + 8 * c1, c1, low2, 0) for c1 in range(2) for side in range(2)]
        for z0 in range(2):
            slot = 13 + 4 * (2 * a1 + z0) + a2
            exponentials(24 + 2 * step + z0, (slot, slot + 2, slot, slot + 2), sizes)
        return carry

    def level0(part, carry):
        pltpu.make_async_copy(xin.at[0, 0], xin.at[0, 0], in_recv.at[part]).wait()
        z0, y0 = group_of(part)
        for slot, y_ref, _ in pairs:
            for c1, c2 in children:
                z = 2 * c1 + z0
                first = xin[slot, 0, z, 2 * c2 + y0]
                second = permute(xin[slot, 1, z, 2 * c2 + 1 - y0], back)
                interpolate(y_ref, 2 * c1 + c2, 2 * c1 + c2, [first, second])
        for slot, y_ref, _ in pairs:
            combine_cores(y_ref, (s0.at[slot, z0, y0, 0], s0.at[slot, z0, 1 - y0, 1]), 2 * part + slot)
        for number, later in ((0, phases1), (1, phases2), (2, phases3)):

            @pl.when(part == number)
            def _(later=later):
                lax.fori_loop(0, 4, later, 0)

        return carry

    lax.fori_loop(0, 4, phases0, 0)
    loads[3].wait()
    lax.fori_loop(0, 4, level0, 0)

    def level1(step):
        a1, a2 = box_of(step)
        for slot, y_ref, _ in pairs:
            for c1, c2 in children:
                blocks = [window(s0.at[slot, c1, c2, side], a1, a2) for side in range(2)]
                interpolate(y_ref, 2 * c1 + c2, 4 + 4 * a2 + 2 * c1 + c2, blocks)
        for slot, y_ref, _ in pairs:
            x1 = x_of(slot)[0]
            combine_cores(y_ref, (z1.at[step, x1, 0], z1.at[step, x1, 1]), 8 + 2 * step + slot)
        pltpu.make_async_remote_copy(
            src_ref=z1.at[step, :, :, :, pl.ds(pl.multiple_of(32 * (1 - core), 8), 40), :],
            dst_ref=zr.at[step],
            send_sem=sib_send.at[step],
            recv_sem=sib_recv.at[step],
            device_id=(bx, my_y * 2 + 1 - core),
            device_id_type=MESH,
        ).start()

    left = lax.broadcasted_iota(jnp.int32, (PAD, LANES), 1) < 64
    left_half = lax.broadcasted_iota(jnp.int32, (HALF, LANES), 1) < 64

    def level23(step):
        a1, a2 = box_of(step)
        y = 2 * a2 + core
        pltpu.make_async_copy(zr.at[0], zr.at[0], sib_recv.at[step]).wait()
        for z0, y_ref, _ in pairs:
            for c1, c2 in children:
                other = zr.at[step, c1, c2]
                blocks = [
                    window(z1.at[step, c1, c2], z0, core),
                    jnp.concatenate([other[z0], other[2 + z0]], axis=0),
                ]
                interpolate(y_ref, 2 * c1 + c2, 4 + 4 * core + 2 * c1 + c2, blocks)
        for z0, y_ref, _ in pairs:
            combine_mirrored(y_ref, (s2.at[z0, 0], s2.at[z0, 1]), 16 + 2 * step + z0, back)
        for z0, y_ref, _ in pairs:
            for c1 in range(2):
                src = s2.at[z0, lax.rem(c1 + core, 2)]
                near, far = [], []
                for x1 in range(2):
                    first = window(src, x1, 0)
                    second = window(src, x1, 1)
                    second = jnp.concatenate([second[4:40], second[36:40], second[44:80], second[76:80]], axis=0)
                    near.append(jnp.where(left, first, pltpu.roll(second, 64, 1)))
                    far.append(jnp.where(left, permute(first, back), permute(second, back_half)))
                interpolate(y_ref, 2 * c1, 4 + 2 * c1, near)
                interpolate(y_ref, 2 * c1 + 1, 4 + 2 * c1 + 1, far)
        for z0, y_ref, acc_ref in pairs:
            z = 2 * a1 + z0
            combine_mirrored(y_ref, (acc_ref.at[0], acc_ref.at[1]), 24 + 2 * step + z0, back_half)
            for x1 in range(2):
                for q1 in range(2):
                    for part in range(2):
                        upper = acc_ref[x1, 2 * part + q1, 0:HALF, :]
                        lower = acc_ref[x1, 2 * part + q1, HALF:ROWS, :]
                        rows = pl.ds(HALF * part, HALF)
                        obuf[step, z0, x1, q1, 0, rows, :] = jnp.where(left_half, upper, pltpu.roll(lower, 64, 1))
                        obuf[step, z0, x1, q1, 1, rows, :] = jnp.where(left_half, pltpu.roll(upper, 64, 1), lower)

            def send_out(target, carry, z=z, z0=z0):
                x1, q1, c = lax.div(target, 4), lax.rem(lax.div(target, 2), 2), lax.rem(target, 2)
                to_bx, to_by = z * 4 + 2 * x1 + q1, 2 * y + c
                src, dst = obuf.at[step, z0, x1, q1, c], orecv.at[chip]
                here = jnp.logical_and(to_bx == bx, to_by == by)

                @pl.when(here)
                def _():
                    pltpu.make_async_copy(src, dst, out_recv.at[step]).start()

                @pl.when(jnp.logical_not(here))
                def _():
                    pltpu.make_async_remote_copy(
                        src_ref=src, dst_ref=dst, send_sem=out_send, recv_sem=out_recv.at[step],
                        device_id=(to_bx, to_by), device_id_type=MESH,
                    ).start()

                return carry

            lax.fori_loop(0, 8, send_out, 0)

    def both(step, carry):
        @pl.when(step < 4)
        def _():
            level1(step)

        @pl.when(step > 0)
        def _():
            level23(step - 1)

        return carry

    lax.fori_loop(0, 5, both, 0)

    def settle(step, carry):
        pltpu.make_async_copy(zr.at[0], zr.at[0], sib_send.at[step]).wait()
        return carry

    lax.fori_loop(0, 4, settle, 0)
    for keeps, sem in ((my_x0 == core, in_send), (lax.rem(my_y, 2) == core, out_send)):

        @pl.when(keeps)
        def _(sem=sem):
            pltpu.make_async_copy(sbuf.at[pl.ds(0, 63)], sbuf.at[pl.ds(0, 63)], sem).wait()

        @pl.when(jnp.logical_not(keeps))
        def _(sem=sem):
            pltpu.make_async_copy(sbuf, sbuf, sem).wait()

    def arrive(step, carry):
        pltpu.make_async_copy(orecv.at[pl.ds(0, 16)], orecv.at[pl.ds(0, 16)], out_recv.at[step]).wait()
        z1_from = lax.rem(lax.div(my_z, 2) + 1 + lax.div(step, 2), 2)
        y1_from = lax.rem(lax.div(my_y, 2) + step, 2)

        def scatter_rows(i, carry):
            z, x, y = 2 * z1_from + lax.div(i, 8), lax.rem(lax.div(i, 2), 4), 2 * y1_from + lax.rem(i, 2)
            ell = z * 16 + x * 4 + y
            for tile in range(9):
                out_ref[pl.ds(tile * 512 + ell, 8, stride=64), :] = orecv[ell, 8 * tile : 8 * tile + 8, :]
            return carry

        lax.fori_loop(0, 16, scatter_rows, 0, unroll=4)
        return carry

    lax.fori_loop(0, 4, arrive, 0)


def shards(coefficients, slowness):
    rows = jnp.transpose(coefficients, (0, 1, 3, 2, 4)).reshape(ROWS * 64, LANES)
    operands = (rows, slowness, jnp.asarray(mixing_tables()), jnp.asarray(row_tables()))
    dense = (ROWS, LANES)
    scratch = [pltpu.VMEM(operands[i].shape, operands[i].dtype) for i in range(4)]
    scratch += [
        pltpu.VMEM(shape, jnp.float32)
        for shape in (
            (64,) + dense,
            (2, 2, 4, 4) + dense,
            (2, 2, 2, 2, 4) + dense,
            (4, 2, 2, 4) + dense,
            (4, 2, 2, 4, 40, LANES),
            (2, 2, 4) + dense,
            (4, 2, 2, 2, 2) + dense,
            (64,) + dense,
            (29, TERMS, LANES),
            (32, 4, 2, TERMS, LANES),
            (4, 2 * TERMS, 2 * LANES),
            (4, 2 * TERMS, 2 * LANES),
            (2, 4) + dense,
            (2, 4) + dense,
        )
    ]
    scratch += [
        pltpu.SemaphoreType.DMA((4,)),
        pltpu.SemaphoreType.DMA,
        pltpu.SemaphoreType.DMA((4,)),
        pltpu.SemaphoreType.DMA((4,)),
        pltpu.SemaphoreType.DMA((4,)),
        pltpu.SemaphoreType.DMA,
        pltpu.SemaphoreType.DMA((4,)),
    ]
    out = pl.pallas_call(
        kernel,
        out_shape=jax.ShapeDtypeStruct((ROWS * 64, LANES), jnp.float32),
        in_specs=[pl.BlockSpec(memory_space=pltpu.HBM)] * 4,
        out_specs=pl.BlockSpec(memory_space=pltpu.VMEM),
        scratch_shapes=scratch,
        compiler_params=pltpu.CompilerParams(has_side_effects=True, vmem_limit_bytes=50 << 20),
    )(*operands)
    return jnp.transpose(out.reshape(2, CHEB, CHEB, 64, LANES), (0, 1, 3, 2, 4))


def solution(mesh):
    placed = (P(None, None, "bx", None, "by"), P())
    return jax.shard_map(
        shards,
        mesh=mesh,
        in_specs=placed,
        out_specs=P(None, None, "bx", None, "by"),
        check_vma=False,
    )
```

time: 115 us -> 99.3 us (0.86)
  Pallas kernels: 110 us -> 91.7 us
  local copies, waits for them, and re-layouts: 4.44 us -> 6.67 us
    pallas_call x1, Pallas kernels: 110 us -> 91.7 us  [shards(): pl.pallas_call(kernel, out_shape=jax.ShapeDtypeStruct((ROWS * 64, LANES),...]
    unnamed x7, local copies, waits for them, and re-layouts: 4.44 us -> 6.67 us
where the time goes in v2:
time: 99.3 us; the launch traced here: 98.4 us
  Pallas kernels  91.7 us (92%)
  local copies, waits for them, and re-layouts  6.67 us (7%)
    pallas_call x1, Pallas kernels, shards(): pl.pallas_call(kernel, out_shape=jax.ShapeDtypeStruct((ROWS * 64, LANES),...  91.7 us
    unnamed x7, local copies, waits for them, and re-layouts  6.67 us

profile of v2, /device:TPU:1, one launch (start us, length us, event | category | flops | bytes accessed | tf_op | source)
XLA Modules:
  0.0 98.4 jit_solution(13585663500368061615)
XLA Ops:
  0.0 0.0 copy-start
  0.0 1.5 %copy-done = bf16[12,288,240]{2,1,0:T(8,128)(2,1)S(1)} copy-done((bf16[12,288,240]{2,1,0:T(8,128)(2,1)S(1)}, bf16[12,288,240]{2,1,0:T(8,128)(2,1)}, u32[]{:S(2)}) %copy-start) | copy-done | bytes 1658904
  1.5 0.0 copy-start.1
  1.5 0.9 copy-done.1
  2.4 0.0 copy-start.2
  2.4 0.9 copy-done.2
  3.3 91.7 %shard_map.46 = f32[4608,128]{1,0:T(8,128)} custom-call(f32[4608,128]{1,0:T(8,128)} %bitcast.7, f32[4,96,96]{2,1,0:T(8,128)S(1)} %copy-done.1, bf16[12,288,240]{2,1,0:T(8,128)(2,1)S(1)} %copy-done, f32[2,144,128]{2,1,0:T(8,128)S(1)} %copy-done.2), custom_call_target="tpu_custom_call" | custom-call | tf_op jit(solution)/shard_map/pallas_call | solution.py:534
  95.0 3.4 %copy.6 = f32[2,6,64,6,128]{4,2,3,1,0:T(8,128)} copy(f32[2,6,64,6,128]{4,2,3,1,0:T(8,128)} %bitcast.6) | data formatting | bytes 4718592
Async XLA Ops:
  0.0 1.5 %copy-start = (bf16[12,288,240]{2,1,0:T(8,128)(2,1)S(1)}, bf16[12,288,240]{2,1,0:T(8,128)(2,1)}, u32[]{:S(2)}) copy-start(bf16[12,288,240]{2,1,0:T(8,128)(2,1)} %constant.4.clone.mix_hbm) | copy-start | bytes 4976644
  1.5 0.9 copy-start.1
  2.4 0.9 copy-start.2

commit v3 on v2

--- a/solution.py
+++ b/solution.py
@@ -1,8 +1,7 @@
-import functools
+import math
 
 import jax
 import jax.numpy as jnp
-import ml_dtypes
 import numpy as np
 from jax import lax
 from jax.experimental import pallas as pl
@@ -15,66 +14,13 @@
 ROWS = 2 * HALF
 TERMS = 4 * HALF
 PAD = 80
+DEPTH = 256
 LANES = 128
 MESH = pl.DeviceIdType.MESH
 
 
 def cheb_points():
     return np.cos(np.pi * (2 * np.arange(CHEB) + 1) / (2 * CHEB))
-
-
-def lagrange_table():
-    points = cheb_points()
-    weights = np.zeros((2, CHEB, CHEB))
-    for quadrant in range(2):
-        shifted = quadrant - 0.5 + points / 2
-        for target in range(CHEB):
-            for source in range(CHEB):
-                product = 1.0
-                for other in range(CHEB):
-                    if other != source:
-                        product = (
-                            product
-                            * (shifted[target] - points[other])
-                            / (points[source] - points[other])
-                        )
-                weights[quadrant, target, source] = product
-    return weights
-
-
-def turns_table():
-    return np.arange(2)[:, None] + (1.0 + cheb_points())[None, :] / 2.0
-
-
-def split16(values):
-    high = values.astype(ml_dtypes.bfloat16)
-    low = (values - high.astype(np.float64)).astype(ml_dtypes.bfloat16)
-    return high, low
-
-
-def mixing_tables():
-    weights = lagrange_table()
-    turns = turns_table()
-    tables = []
-    for parts in ((0, HALF), (0, 40), (4, 44)):
-        for c1, c2 in ((0, 0), (0, 1), (1, 0), (1, 1)):
-            w1 = weights * np.exp(2j * np.pi * (c1 - 0.5) * turns)[:, :, None]
-            w2 = weights * np.exp(2j * np.pi * (c2 - 0.5) * turns)[:, :, None]
-            full = np.einsum("qts,puv->qptusv", w1, w2).reshape(TERMS, HALF)
-            real = np.zeros((2 * TERMS, PAD))
-            real[:, parts[0] : parts[0] + HALF] = np.concatenate([full.real, full.imag])
-            real[:, parts[1] : parts[1] + HALF] = np.concatenate([-full.imag, full.real])
-            high, low = split16(real)
-            tables.append(np.concatenate([high, high, low], axis=1))
-    return np.stack(tables)
-
-
-def row_tables():
-    q1, q2, t1, t2 = [
-        axis.reshape(-1) for axis in np.meshgrid(*[np.arange(n) for n in (2, 2, CHEB, CHEB)], indexing="ij")
-    ]
-    rows = np.stack([CHEB * q1 + t1, CHEB * q2 + t2])
-    return np.broadcast_to(rows[:, :, None], (2, TERMS, LANES)).astype(np.float32)
 
 
 def fit(function, degree):
@@ -84,8 +30,15 @@
     return [float(c) for c in series.convert(kind=np.polynomial.Polynomial).coef]
 
 
-SIN = fit(lambda r: np.sin(2 * np.pi * r) / r, 5)
-COS = fit(lambda r: np.cos(2 * np.pi * r), 5)
+SIN = fit(lambda r: math.sqrt(2) * np.sin(np.pi * r) / r, 3)
+COS = fit(lambda r: math.sqrt(2) * np.cos(np.pi * r), 4)
+WHOLE = 1.5 * 2.0**23
+
+
+POINTS = [float(point) for point in cheb_points()]
+SCALES = [
+    float(1 / np.prod([cheb_points()[s] - cheb_points()[j] for j in range(CHEB) if j != s])) for s in range(CHEB)
+]
 
 
 def horner(coefficients, s):
@@ -96,9 +49,10 @@
 
 
 def unit(turns):
-    r = turns - jnp.round(turns)
+    r = turns - ((turns + WHOLE) - WHOLE)
     s = r * r
-    return horner(COS, s), horner(SIN, s) * r
+    half = horner(SIN, s) * r
+    return 1.0 - half * half, half * horner(COS, s)
 
 
 def operand(block):
@@ -106,7 +60,74 @@
         block = jnp.concatenate([block, jnp.zeros((PAD - block.shape[0], block.shape[1]), jnp.float32)], axis=0)
     high = block.astype(jnp.bfloat16)
     low = (block - high.astype(jnp.float32)).astype(jnp.bfloat16)
-    return jnp.concatenate([high, low, high], axis=0)
+    return jnp.concatenate([high, low, high, jnp.zeros((DEPTH - 3 * PAD, block.shape[1]), jnp.bfloat16)], axis=0)
+
+
+def choose(index, values):
+    result = jnp.full(index.shape, values[0], jnp.float32)
+    for number, value in enumerate(values[1:], 1):
+        result = jnp.where(index == number, value, result)
+    return result
+
+
+def digits(value, *sizes):
+    out = []
+    for size in sizes[::-1]:
+        rest = jnp.floor((value + 0.5) * (1.0 / size))
+        out.append(value - rest * size)
+        value = rest
+    return out[::-1]
+
+
+def lagrange(at, source):
+    product = choose(source, SCALES)
+    for number, point in enumerate(POINTS):
+        product = product * jnp.where(source == number, 1.0, at - point)
+    return product
+
+
+def mixing_tables(mix_ref, raw_ref):
+    shape = (HALF, DEPTH)
+    column = lax.broadcasted_iota(jnp.int32, shape, 1).astype(jnp.float32)
+    copy, inside = digits(column, 4, PAD)
+    row = lax.broadcasted_iota(jnp.int32, shape, 0).astype(jnp.float32)
+    t1, t2 = digits(row, CHEB, CHEB)
+    second = inside >= 40
+    place = inside - jnp.where(second, 40.0, 0.0)
+    used = jnp.logical_and(place < HALF, copy < 3)
+    s1, s2 = digits(jnp.minimum(place, HALF - 1.0), CHEB, CHEB)
+    at1, at2 = choose(t1, POINTS) * 0.5, choose(t2, POINTS) * 0.5
+    weights1 = [jnp.where(used, lagrange(q - 0.5 + at1, s1), 0.0) for q in range(2)]
+    weights2 = [lagrange(q - 0.5 + at2, s2) for q in range(2)]
+    for q1 in range(2):
+        for q2 in range(2):
+            weights = weights1[q1] * weights2[q2]
+            turns1, turns2 = 0.5 * (q1 + 0.5 + at1), 0.5 * (q2 + 0.5 + at2)
+            plus, minus = unit(turns1 + turns2), unit(turns1 - turns2)
+            for c1 in range(2):
+                for c2 in range(2):
+                    co, si = plus if c1 == c2 else minus
+                    si = si if c1 else -si
+                    real, imag = co * weights, si * weights
+                    for part, values in enumerate((jnp.where(second, -imag, real), jnp.where(second, real, imag))):
+                        high = values.astype(jnp.bfloat16).astype(jnp.float32)
+                        values = jnp.where(copy < 2, high, values - high)
+                        base = part * TERMS + q1 * ROWS + q2 * HALF
+                        raw_ref[2 * c1 + c2, base : base + HALF, :] = values
+
+    shape = (48, DEPTH)
+    copy, inside = digits(lax.broadcasted_iota(jnp.int32, shape, 1).astype(jnp.float32), 4, PAD)
+
+    def variants(i, carry):
+        table, rows = lax.div(i, 6), pl.ds(pl.multiple_of(48 * lax.rem(i, 6), 16), 48)
+        values = raw_ref[table, rows, :]
+        dense = jnp.where(inside < HALF, values, pltpu.roll(values, DEPTH - 4, 1))
+        dense = jnp.where(inside < ROWS, dense, 0.0)
+        for variant, block in enumerate((dense, values, pltpu.roll(values, 4, 1))):
+            mix_ref[4 * variant + table, rows, :] = block.astype(jnp.bfloat16)
+        return carry
+
+    lax.fori_loop(0, 24, variants, 0)
 
 
 def reverse6(value):
@@ -117,8 +138,8 @@
 
 
 def kernel(
-    coef_hbm, slow_hbm, mix_hbm, rows_hbm, out_ref,
-    coef_ref, slow_ref, mix_ref, rows_ref,
+    coef_hbm, slow_hbm, out_ref,
+    coef_ref, slow_ref, mix_ref, raw_ref,
     sbuf, xin, s0, z1, zr, s2, obuf, orecv, vtab, e_tab, y_a, y_b, acc_a, acc_b,
     load, in_send, in_recv, sib_send, sib_recv, out_send, out_recv,
 ):
@@ -132,12 +153,30 @@
     loads = [
         pltpu.make_async_copy(src, dst, load.at[i])
         for i, (src, dst) in enumerate(
-            ((coef_hbm, coef_ref), (slow_hbm, slow_ref), (rows_hbm, rows_ref), (mix_hbm, mix_ref))
+            ((coef_hbm, coef_ref), (slow_hbm, slow_ref))
         )
     ]
     for copy in loads:
         copy.start()
+
+    barrier = pltpu.get_barrier_semaphore()
+    me = bx * 8 + by
+
+    def greet(i, carry):
+        there = lax.rem(me + i, 128)
+        pl.semaphore_signal(barrier, inc=1, device_id=(lax.div(there, 8), lax.rem(there, 8)), device_id_type=MESH)
+        return carry
+
+    lax.fori_loop(1, 128, greet, 0)
     loads[0].wait()
+
+    def gather_rows(ell, carry):
+        for tile in range(9):
+            sbuf[ell, 8 * tile : 8 * tile + 8, :] = coef_ref[pl.ds(tile * 512 + ell, 8, stride=64), :]
+        return carry
+
+    lax.fori_loop(0, 64, gather_rows, 0, unroll=8)
+    pl.semaphore_wait(barrier, 127)
 
     def send_in(step, carry):
         part, inner = lax.div(step, 16), lax.rem(step, 16)
@@ -150,8 +189,6 @@
         to_x, to_z, to_y = lax.rem(my_x + dx, 4), lax.rem(my_z + dz, 4), lax.rem(my_y + dy, 4)
         to_bx, to_by = to_z * 4 + to_x, to_y * 2 + my_x0
         ell = to_z * 16 + to_x * 4 + to_y
-        for tile in range(9):
-            sbuf[ell, 8 * tile : 8 * tile + 8, :] = coef_ref[pl.ds(tile * 512 + ell, 8, stride=64), :]
         src = sbuf.at[ell]
         dst = xin.at[lax.div(dx, 2), core, my_z, my_y]
         here = jnp.logical_and(to_bx == bx, to_by == by)
@@ -172,10 +209,10 @@
     lax.fori_loop(0, 64, send_in, 0)
 
     loads[1].wait()
-    loads[2].wait()
     lane = lax.broadcasted_iota(jnp.int32, (TERMS, 96), 1).astype(jnp.float32)
-    row_i = rows_ref[0, :, 0:96]
-    row_j = rows_ref[1, :, 0:96]
+    row = lax.broadcasted_iota(jnp.int32, (TERMS, 96), 0).astype(jnp.float32)
+    q1, q2, t1, t2 = digits(row, 2, 2, CHEB, CHEB)
+    row_i, row_j = CHEB * q1 + t1, CHEB * q2 + t2
 
     def spread(level, a1):
         pick = jnp.where(row_i + (12 * a1).astype(jnp.float32) == lane, 1.0, 0.0)
@@ -312,7 +349,7 @@
         return lax.rem(my_z + lax.div(part, 2), 2), lax.rem(my_y + lax.rem(part, 2), 2)
 
     def box_of(step):
-        return lax.rem(lax.div(my_z, 2) + 1 + lax.div(step, 2), 2), lax.rem(lax.div(my_y, 2) + step, 2)
+        return lax.rem(lax.div(my_z, 2) + 1 + lax.div(step, 2), 2), lax.rem(lax.div(my_y, 2) + 1 + step, 2)
 
     children = [(c1, c2) for c1 in range(2) for c2 in range(2)]
 
@@ -369,7 +406,7 @@
         return carry
 
     lax.fori_loop(0, 4, phases0, 0)
-    loads[3].wait()
+    mixing_tables(mix_ref, raw_ref)
     lax.fori_loop(0, 4, level0, 0)
 
     def level1(step):
@@ -397,7 +434,10 @@
         a1, a2 = box_of(step)
         y = 2 * a2 + core
         pltpu.make_async_copy(zr.at[0], zr.at[0], sib_recv.at[step]).wait()
-        for z0, y_ref, _ in pairs:
+        near_z0 = lax.rem(my_z, 2)
+        z0_of = (near_z0, 1 - near_z0)
+        for i, y_ref, _ in pairs:
+            z0 = z0_of[i]
             for c1, c2 in children:
                 other = zr.at[step, c1, c2]
                 blocks = [
@@ -405,11 +445,11 @@
                     jnp.concatenate([other[z0], other[2 + z0]], axis=0),
                 ]
                 interpolate(y_ref, 2 * c1 + c2, 4 + 4 * core + 2 * c1 + c2, blocks)
-        for z0, y_ref, _ in pairs:
-            combine_mirrored(y_ref, (s2.at[z0, 0], s2.at[z0, 1]), 16 + 2 * step + z0, back)
-        for z0, y_ref, _ in pairs:
+        for i, y_ref, _ in pairs:
+            combine_mirrored(y_ref, (s2.at[i, 0], s2.at[i, 1]), 16 + 2 * step + z0_of[i], back)
+        for i, y_ref, _ in pairs:
             for c1 in range(2):
-                src = s2.at[z0, lax.rem(c1 + core, 2)]
+                src = s2.at[i, lax.rem(c1 + core, 2)]
                 near, far = [], []
                 for x1 in range(2):
                     first = window(src, x1, 0)
@@ -419,7 +459,8 @@
                     far.append(jnp.where(left, permute(first, back), permute(second, back_half)))
                 interpolate(y_ref, 2 * c1, 4 + 2 * c1, near)
                 interpolate(y_ref, 2 * c1 + 1, 4 + 2 * c1 + 1, far)
-        for z0, y_ref, acc_ref in pairs:
+        for i, y_ref, acc_ref in pairs:
+            z0 = z0_of[i]
             z = 2 * a1 + z0
             combine_mirrored(y_ref, (acc_ref.at[0], acc_ref.at[1]), 24 + 2 * step + z0, back_half)
             for x1 in range(2):
@@ -428,13 +469,15 @@
                         upper = acc_ref[x1, 2 * part + q1, 0:HALF, :]
                         lower = acc_ref[x1, 2 * part + q1, HALF:ROWS, :]
                         rows = pl.ds(HALF * part, HALF)
-                        obuf[step, z0, x1, q1, 0, rows, :] = jnp.where(left_half, upper, pltpu.roll(lower, 64, 1))
-                        obuf[step, z0, x1, q1, 1, rows, :] = jnp.where(left_half, pltpu.roll(upper, 64, 1), lower)
-
-            def send_out(target, carry, z=z, z0=z0):
-                x1, q1, c = lax.div(target, 4), lax.rem(lax.div(target, 2), 2), lax.rem(target, 2)
-                to_bx, to_by = z * 4 + 2 * x1 + q1, 2 * y + c
-                src, dst = obuf.at[step, z0, x1, q1, c], orecv.at[chip]
+                        obuf[step, i, x1, q1, 0, rows, :] = jnp.where(left_half, upper, pltpu.roll(lower, 64, 1))
+                        obuf[step, i, x1, q1, 1, rows, :] = jnp.where(left_half, pltpu.roll(upper, 64, 1), lower)
+
+            def send_out(target, carry, z=z, i=i):
+                hop = lax.div(target, 2)
+                x = lax.rem(my_x + 5 + 2 * core + hop, 4)
+                c = lax.rem(target + core, 2)
+                to_bx, to_by = z * 4 + x, 2 * y + c
+                src, dst = obuf.at[step, i, lax.div(x, 2), lax.rem(x, 2), c], orecv.at[chip]
                 here = jnp.logical_and(to_bx == bx, to_by == by)
 
                 @pl.when(here)
@@ -483,7 +526,7 @@
     def arrive(step, carry):
         pltpu.make_async_copy(orecv.at[pl.ds(0, 16)], orecv.at[pl.ds(0, 16)], out_recv.at[step]).wait()
         z1_from = lax.rem(lax.div(my_z, 2) + 1 + lax.div(step, 2), 2)
-        y1_from = lax.rem(lax.div(my_y, 2) + step, 2)
+        y1_from = lax.rem(lax.div(my_y, 2) + 1 + step, 2)
 
         def scatter_rows(i, carry):
             z, x, y = 2 * z1_from + lax.div(i, 8), lax.rem(lax.div(i, 2), 4), 2 * y1_from + lax.rem(i, 2)
@@ -500,9 +543,10 @@
 
 def shards(coefficients, slowness):
     rows = jnp.transpose(coefficients, (0, 1, 3, 2, 4)).reshape(ROWS * 64, LANES)
-    operands = (rows, slowness, jnp.asarray(mixing_tables()), jnp.asarray(row_tables()))
+    operands = (rows, slowness)
     dense = (ROWS, LANES)
-    scratch = [pltpu.VMEM(operands[i].shape, operands[i].dtype) for i in range(4)]
+    scratch = [pltpu.VMEM(operands[i].shape, jnp.float32) for i in range(2)]
+    scratch += [pltpu.VMEM((12, 2 * TERMS, DEPTH), jnp.bfloat16), pltpu.VMEM((4, 2 * TERMS, DEPTH), jnp.float32)]
     scratch += [
         pltpu.VMEM(shape, jnp.float32)
         for shape in (
@@ -534,10 +578,10 @@
     out = pl.pallas_call(
         kernel,
         out_shape=jax.ShapeDtypeStruct((ROWS * 64, LANES), jnp.float32),
-        in_specs=[pl.BlockSpec(memory_space=pltpu.HBM)] * 4,
+        in_specs=[pl.BlockSpec(memory_space=pl.ANY)] * 2,
         out_specs=pl.BlockSpec(memory_space=pltpu.VMEM),
         scratch_shapes=scratch,
-        compiler_params=pltpu.CompilerParams(has_side_effects=True, vmem_limit_bytes=50 << 20),
+        compiler_params=pltpu.CompilerParams(collective_id=0, has_side_effects=True, vmem_limit_bytes=50 << 20),
     )(*operands)
     return jnp.transpose(out.reshape(2, CHEB, CHEB, 64, LANES), (0, 1, 3, 2, 4))
 

time: 99.3 us -> 87.9 us (0.89)
  Pallas kernels: 91.7 us -> 85.1 us
  local copies, waits for them, and re-layouts: 6.67 us -> 2.33 us
    pallas_call x1, Pallas kernels: 91.7 us -> 85.1 us  [shards(): pl.pallas_call(kernel, out_shape=jax.ShapeDtypeStruct((ROWS * 64, LANES),...]
    unnamed x7 -> x3, local copies, waits for them, and re-layouts: 6.67 us -> 2.33 us
where the time goes in v3:
time: 87.9 us; the launch traced here: 87.5 us
  Pallas kernels  85.1 us (97%)
  local copies, waits for them, and re-layouts  2.33 us (3%)
    pallas_call x1, Pallas kernels, shards(): pl.pallas_call(kernel, out_shape=jax.ShapeDtypeStruct((ROWS * 64, LANES),...  85.1 us
    unnamed x3, local copies, waits for them, and re-layouts  2.33 us

profile of v3, /device:TPU:1, one launch (start us, length us, event | category | flops | bytes accessed | tf_op | source)
XLA Modules:
  0.0 87.5 jit_solution(2097068852889229226)
XLA Ops:
  0.0 0.0 copy-start
  0.0 0.9 %copy-done = f32[4,96,96]{2,1,0:T(8,128)S(1)} copy-done((f32[4,96,96]{2,1,0:T(8,128)S(1)}, f32[4,96,96]{2,1,0:T(8,128)}, u32[]{:S(2)}) %copy-start) | copy-done | bytes 147480
  0.9 85.1 %shard_map.28 = f32[4608,128]{1,0:T(8,128)S(1)} custom-call(f32[4608,128]{1,0:T(8,128)} %bitcast.7, f32[4,96,96]{2,1,0:T(8,128)S(1)} %copy-done), custom_call_target="tpu_custom_call" | custom-call | tf_op jit(solution)/shard_map/pallas_call | solution.py:578
  86.1 1.4 %copy.4 = f32[2,6,64,6,128]{4,2,3,1,0:T(8,128)} copy(f32[2,6,64,6,128]{4,2,3,1,0:T(8,128)S(1)} %bitcast.6) | data formatting | bytes 4718592
Async XLA Ops:
  0.0 0.9 %copy-start = (f32[4,96,96]{2,1,0:T(8,128)S(1)}, f32[4,96,96]{2,1,0:T(8,128)}, u32[]{:S(2)}) copy-start(f32[4,96,96]{2,1,0:T(8,128)} %slow_hbm.1) | copy-start | bytes 442372

commit v4 on v3

--- a/solution.py
+++ b/solution.py
@@ -179,13 +179,11 @@
     pl.semaphore_wait(barrier, 127)
 
     def send_in(step, carry):
-        part, inner = lax.div(step, 16), lax.rem(step, 16)
-        pz, py = lax.div(part, 2), lax.rem(lax.rem(part, 2) + core, 2)
-        other = lax.div(inner, 4)
-        dx = lax.rem(lax.rem(inner, 4) + other, 4)
-        dz, dy = 2 * lax.div(other, 2) + pz, 2 * lax.rem(other, 2) + py
-        sign = 1 - 2 * core
-        dx, dz, dy = [lax.rem(4 + sign * d, 4) for d in (dx, dz, dy)]
+        half, inner = lax.div(step, 32), lax.rem(step, 32)
+        dx, group = lax.rem(inner, 4), lax.div(inner, 4)
+        dy = lax.rem(dx + group, 4)
+        dz = half + 2 * lax.rem(lax.div(group, 4) + dx, 2)
+        dx, dz, dy = [lax.rem(d + 2 * core, 4) for d in (dx, dz, dy)]
         to_x, to_z, to_y = lax.rem(my_x + dx, 4), lax.rem(my_z + dz, 4), lax.rem(my_y + dy, 4)
         to_bx, to_by = to_z * 4 + to_x, to_y * 2 + my_x0
         ell = to_z * 16 + to_x * 4 + to_y
@@ -195,12 +193,12 @@
 
         @pl.when(here)
         def _():
-            pltpu.make_async_copy(src, dst, in_recv.at[part]).start()
+            pltpu.make_async_copy(src, dst, in_recv.at[half]).start()
 
         @pl.when(jnp.logical_not(here))
         def _():
             pltpu.make_async_remote_copy(
-                src_ref=src, dst_ref=dst, send_sem=in_send, recv_sem=in_recv.at[part],
+                src_ref=src, dst_ref=dst, send_sem=in_send, recv_sem=in_recv.at[half],
                 device_id=(to_bx, to_by), device_id_type=MESH,
             ).start()
 
@@ -345,16 +343,18 @@
         x = lax.rem(my_x - dx + 4, 4)
         return lax.div(x, 2), low1 + 4 * lax.div(x, 2) + 8 * core
 
-    def group_of(part):
-        return lax.rem(my_z + lax.div(part, 2), 2), lax.rem(my_y + lax.rem(part, 2), 2)
-
-    def box_of(step):
-        return lax.rem(lax.div(my_z, 2) + 1 + lax.div(step, 2), 2), lax.rem(lax.div(my_y, 2) + 1 + step, 2)
+    def box_of(box):
+        other1 = 1 - lax.rem(box, 2)
+        other2 = 1 - lax.rem(lax.rem(box, 2) + lax.div(box, 2), 2)
+        return lax.rem(lax.div(my_z, 2) + other1, 2), lax.rem(lax.div(my_y, 2) + other2, 2)
+
+    def turn_of(step, on_core):
+        return step + on_core * (1 - 2 * lax.rem(step, 2))
 
     children = [(c1, c2) for c1 in range(2) for c2 in range(2)]
 
     def phases0(part, carry):
-        z0, y0 = group_of(part)
+        z0, y0 = lax.rem(my_z + lax.div(part, 2), 2), lax.rem(part, 2)
         for slot in range(2):
             r1 = x_of(slot)[1] + 2 * z0
             sizes = [magnitude(0, r1 + c1, c1, lane2 + (c2 + 2 * y0), c2) for c1, c2 in children]
@@ -387,8 +387,7 @@
         return carry
 
     def level0(part, carry):
-        pltpu.make_async_copy(xin.at[0, 0], xin.at[0, 0], in_recv.at[part]).wait()
-        z0, y0 = group_of(part)
+        z0, y0 = lax.rem(my_z + lax.div(part, 2), 2), lax.rem(part, 2)
         for slot, y_ref, _ in pairs:
             for c1, c2 in children:
                 z = 2 * c1 + z0
@@ -397,17 +396,23 @@
                 interpolate(y_ref, 2 * c1 + c2, 2 * c1 + c2, [first, second])
         for slot, y_ref, _ in pairs:
             combine_cores(y_ref, (s0.at[slot, z0, y0, 0], s0.at[slot, z0, 1 - y0, 1]), 2 * part + slot)
-        for number, later in ((0, phases1), (1, phases2), (2, phases3)):
-
-            @pl.when(part == number)
-            def _(later=later):
-                lax.fori_loop(0, 4, later, 0)
-
-        return carry
-
-    lax.fori_loop(0, 4, phases0, 0)
+        return carry
+
     mixing_tables(mix_ref, raw_ref)
-    lax.fori_loop(0, 4, level0, 0)
+    for phases in (phases0, phases1, phases2):
+        lax.fori_loop(0, 4, phases, 0)
+
+    def arrived(half, carry):
+        pltpu.make_async_copy(xin.at[0], xin.at[0], in_recv.at[half]).wait()
+        lax.fori_loop(2 * half, 2 * half + 2, level0, 0)
+
+        @pl.when(half == 0)
+        def _():
+            lax.fori_loop(0, 4, phases3, 0)
+
+        return carry
+
+    lax.fori_loop(0, 2, arrived, 0)
 
     def level1(step):
         a1, a2 = box_of(step)
@@ -502,7 +507,7 @@
 
         @pl.when(step > 0)
         def _():
-            level23(step - 1)
+            level23(turn_of(step - 1, core))
 
         return carry
 
@@ -524,9 +529,9 @@
             pltpu.make_async_copy(sbuf, sbuf, sem).wait()
 
     def arrive(step, carry):
-        pltpu.make_async_copy(orecv.at[pl.ds(0, 16)], orecv.at[pl.ds(0, 16)], out_recv.at[step]).wait()
-        z1_from = lax.rem(lax.div(my_z, 2) + 1 + lax.div(step, 2), 2)
-        y1_from = lax.rem(lax.div(my_y, 2) + 1 + step, 2)
+        box = turn_of(step, lax.rem(my_y, 2))
+        pltpu.make_async_copy(orecv.at[pl.ds(0, 16)], orecv.at[pl.ds(0, 16)], out_recv.at[box]).wait()
+        z1_from, y1_from = box_of(box)
 
         def scatter_rows(i, carry):
             z, x, y = 2 * z1_from + lax.div(i, 8), lax.rem(lax.div(i, 2), 4), 2 * y1_from + lax.rem(i, 2)
@@ -569,7 +574,7 @@
     scratch += [
         pltpu.SemaphoreType.DMA((4,)),
         pltpu.SemaphoreType.DMA,
-        pltpu.SemaphoreType.DMA((4,)),
+        pltpu.SemaphoreType.DMA((2,)),
         pltpu.SemaphoreType.DMA((4,)),
         pltpu.SemaphoreType.DMA((4,)),
         pltpu.SemaphoreType.DMA,

time: 87.9 us -> 85 us (0.967)
  Pallas kernels: 85.1 us -> 82.5 us
    pallas_call x1, Pallas kernels: 85.1 us -> 82.5 us  [shards(): pl.pallas_call(kernel, out_shape=jax.ShapeDtypeStruct((ROWS * 64, LANES),...]
where the time goes in v4:
time: 85 us; the launch traced here: 84.9 us
  Pallas kernels  82.5 us (97%)
  local copies, waits for them, and re-layouts  2.33 us (3%)
    pallas_call x1, Pallas kernels, shards(): pl.pallas_call(kernel, out_shape=jax.ShapeDtypeStruct((ROWS * 64, LANES),...  82.5 us
    unnamed x3, local copies, waits for them, and re-layouts  2.33 us

profile of v4, /device:TPU:1, one launch (start us, length us, event | category | flops | bytes accessed | tf_op | source)
XLA Modules:
  0.0 84.9 jit_solution(10318932692141084617)
XLA Ops:
  0.0 0.0 copy-start
  0.0 0.9 %copy-done = f32[4,96,96]{2,1,0:T(8,128)S(1)} copy-done((f32[4,96,96]{2,1,0:T(8,128)S(1)}, f32[4,96,96]{2,1,0:T(8,128)}, u32[]{:S(2)}) %copy-start) | copy-done | bytes 147480
  0.9 82.5 %shard_map.28 = f32[4608,128]{1,0:T(8,128)S(1)} custom-call(f32[4608,128]{1,0:T(8,128)} %bitcast.7, f32[4,96,96]{2,1,0:T(8,128)S(1)} %copy-done), custom_call_target="tpu_custom_call" | custom-call | tf_op jit(solution)/shard_map/pallas_call | solution.py:583
  83.4 1.4 %copy.4 = f32[2,6,64,6,128]{4,2,3,1,0:T(8,128)} copy(f32[2,6,64,6,128]{4,2,3,1,0:T(8,128)S(1)} %bitcast.6) | data formatting | bytes 4718592
Async XLA Ops:
  0.0 0.9 %copy-start = (f32[4,96,96]{2,1,0:T(8,128)S(1)}, f32[4,96,96]{2,1,0:T(8,128)}, u32[]{:S(2)}) copy-start(f32[4,96,96]{2,1,0:T(8,128)} %slow_hbm.1) | copy-start | bytes 442372

commit v5 on v4

--- a/solution.py
+++ b/solution.py
@@ -167,7 +167,8 @@
         pl.semaphore_signal(barrier, inc=1, device_id=(lax.div(there, 8), lax.rem(there, 8)), device_id_type=MESH)
         return carry
 
-    lax.fori_loop(1, 128, greet, 0)
+    lax.fori_loop(1, 121, greet, 0, unroll=8)
+    lax.fori_loop(121, 128, greet, 0, unroll=7)
     loads[0].wait()
 
     def gather_rows(ell, carry):
@@ -348,8 +349,11 @@
         other2 = 1 - lax.rem(lax.rem(box, 2) + lax.div(box, 2), 2)
         return lax.rem(lax.div(my_z, 2) + other1, 2), lax.rem(lax.div(my_y, 2) + other2, 2)
 
+    def order_of(step):
+        return step + lax.div(step, 2) * (1 - 2 * lax.rem(step, 2))
+
     def turn_of(step, on_core):
-        return step + on_core * (1 - 2 * lax.rem(step, 2))
+        return order_of(step + on_core * (1 - 2 * lax.rem(step, 2)))
 
     children = [(c1, c2) for c1 in range(2) for c2 in range(2)]
 
@@ -436,8 +440,6 @@
     left_half = lax.broadcasted_iota(jnp.int32, (HALF, LANES), 1) < 64
 
     def level23(step):
-        a1, a2 = box_of(step)
-        y = 2 * a2 + core
         pltpu.make_async_copy(zr.at[0], zr.at[0], sib_recv.at[step]).wait()
         near_z0 = lax.rem(my_z, 2)
         z0_of = (near_z0, 1 - near_z0)
@@ -465,9 +467,7 @@
                 interpolate(y_ref, 2 * c1, 4 + 2 * c1, near)
                 interpolate(y_ref, 2 * c1 + 1, 4 + 2 * c1 + 1, far)
         for i, y_ref, acc_ref in pairs:
-            z0 = z0_of[i]
-            z = 2 * a1 + z0
-            combine_mirrored(y_ref, (acc_ref.at[0], acc_ref.at[1]), 24 + 2 * step + z0, back_half)
+            combine_mirrored(y_ref, (acc_ref.at[0], acc_ref.at[1]), 24 + 2 * step + z0_of[i], back_half)
             for x1 in range(2):
                 for q1 in range(2):
                     for part in range(2):
@@ -477,41 +477,50 @@
                         obuf[step, i, x1, q1, 0, rows, :] = jnp.where(left_half, upper, pltpu.roll(lower, 64, 1))
                         obuf[step, i, x1, q1, 1, rows, :] = jnp.where(left_half, pltpu.roll(upper, 64, 1), lower)
 
-            def send_out(target, carry, z=z, i=i):
-                hop = lax.div(target, 2)
-                x = lax.rem(my_x + 5 + 2 * core + hop, 4)
-                c = lax.rem(target + core, 2)
-                to_bx, to_by = z * 4 + x, 2 * y + c
-                src, dst = obuf.at[step, i, lax.div(x, 2), lax.rem(x, 2), c], orecv.at[chip]
-                here = jnp.logical_and(to_bx == bx, to_by == by)
-
-                @pl.when(here)
-                def _():
-                    pltpu.make_async_copy(src, dst, out_recv.at[step]).start()
-
-                @pl.when(jnp.logical_not(here))
-                def _():
-                    pltpu.make_async_remote_copy(
-                        src_ref=src, dst_ref=dst, send_sem=out_send, recv_sem=out_recv.at[step],
-                        device_id=(to_bx, to_by), device_id_type=MESH,
-                    ).start()
-
-                return carry
-
-            lax.fori_loop(0, 8, send_out, 0)
+    def send_out(box, number):
+        i, hop, later = lax.rem(number, 2), lax.div(number, 2), lax.div(number, 8)
+        a1, a2 = box_of(box)
+        x = lax.rem(my_x + 1 + 2 * core + hop, 4)
+        c = lax.rem(later + core, 2)
+        to_bx, to_by = (2 * a1 + lax.rem(my_z + i, 2)) * 4 + x, 2 * (2 * a2 + core) + c
+        src, dst = obuf.at[box, i, lax.div(x, 2), lax.rem(x, 2), c], orecv.at[chip]
+        here = jnp.logical_and(to_bx == bx, to_by == by)
+
+        @pl.when(here)
+        def _():
+            pltpu.make_async_copy(src, dst, out_recv.at[box]).start()
+
+        @pl.when(jnp.logical_not(here))
+        def _():
+            pltpu.make_async_remote_copy(
+                src_ref=src, dst_ref=dst, send_sem=out_send, recv_sem=out_recv.at[box],
+                device_id=(to_bx, to_by), device_id_type=MESH,
+            ).start()
 
     def both(step, carry):
         @pl.when(step < 4)
         def _():
-            level1(step)
-
-        @pl.when(step > 0)
+            level1(order_of(step))
+
+        @pl.when(jnp.logical_and(step > 0, step < 5))
         def _():
             level23(turn_of(step - 1, core))
 
-        return carry
-
-    lax.fori_loop(0, 5, both, 0)
+        def send_some(number, carry):
+            @pl.when(jnp.logical_and(step > 0, step < 5))
+            def _():
+                send_out(turn_of(step - 1, core), number)
+
+            @pl.when(step > 1)
+            def _():
+                send_out(turn_of(step - 2, core), number + 8)
+
+            return carry
+
+        lax.fori_loop(0, 8, send_some, 0)
+        return carry
+
+    lax.fori_loop(0, 6, both, 0)
 
     def settle(step, carry):
         pltpu.make_async_copy(zr.at[0], zr.at[0], sib_send.at[step]).wait()
@@ -548,7 +557,7 @@
 
 def shards(coefficients, slowness):
     rows = jnp.transpose(coefficients, (0, 1, 3, 2, 4)).reshape(ROWS * 64, LANES)
-    operands = (rows, slowness)
+    operands = (rows, pltpu.with_memory_space_constraint(slowness, pltpu.HBM))
     dense = (ROWS, LANES)
     scratch = [pltpu.VMEM(operands[i].shape, jnp.float32) for i in range(2)]
     scratch += [pltpu.VMEM((12, 2 * TERMS, DEPTH), jnp.bfloat16), pltpu.VMEM((4, 2 * TERMS, DEPTH), jnp.float32)]
@@ -583,7 +592,7 @@
     out = pl.pallas_call(
         kernel,
         out_shape=jax.ShapeDtypeStruct((ROWS * 64, LANES), jnp.float32),
-        in_specs=[pl.BlockSpec(memory_space=pl.ANY)] * 2,
+        in_specs=[pl.BlockSpec(memory_space=pl.ANY), pl.BlockSpec(memory_space=pltpu.HBM)],
         out_specs=pl.BlockSpec(memory_space=pltpu.VMEM),
         scratch_shapes=scratch,
         compiler_params=pltpu.CompilerParams(collective_id=0, has_side_effects=True, vmem_limit_bytes=50 << 20),

time: 85 us -> 80.8 us (0.951)
  Pallas kernels: 82.5 us -> 78.6 us
  local copies, waits for them, and re-layouts: 2.33 us -> 1.41 us
    pallas_call x1, Pallas kernels: 82.5 us -> 78.6 us  [shards(): pl.pallas_call(kernel, out_shape=jax.ShapeDtypeStruct((ROWS * 64, LANES),...]
    unnamed x3 -> x1, local copies, waits for them, and re-layouts: 2.33 us -> 1.41 us
where the time goes in v5:
time: 80.8 us; the launch traced here: 80.1 us
  Pallas kernels  78.6 us (97%)
  local copies, waits for them, and re-layouts  1.41 us (2%)
    pallas_call x1, Pallas kernels, shards(): pl.pallas_call(kernel, out_shape=jax.ShapeDtypeStruct((ROWS * 64, LANES),...  78.6 us

profile of v5, /device:TPU:1, one launch (start us, length us, event | category | flops | bytes accessed | tf_op | source)
XLA Modules:
  0.0 80.1 jit_solution(14357636545031783122)
XLA Ops:
  0.0 78.6 %shard_map.28 = f32[4608,128]{1,0:T(8,128)S(1)} custom-call(f32[4608,128]{1,0:T(8,128)} %bitcast.7, f32[4,96,96]{2,1,0:T(8,128)} %slow_hbm.1), custom_call_target="tpu_custom_call" | custom-call | tf_op jit(solution)/shard_map/pallas_call | solution.py:592
  78.7 1.4 %copy.4 = f32[2,6,64,6,128]{4,2,3,1,0:T(8,128)} copy(f32[2,6,64,6,128]{4,2,3,1,0:T(8,128)S(1)} %bitcast.6) | data formatting | bytes 4718592

commit v6 on v5

--- a/solution.py
+++ b/solution.py
@@ -348,12 +348,6 @@
         other1 = 1 - lax.rem(box, 2)
         other2 = 1 - lax.rem(lax.rem(box, 2) + lax.div(box, 2), 2)
         return lax.rem(lax.div(my_z, 2) + other1, 2), lax.rem(lax.div(my_y, 2) + other2, 2)
-
-    def order_of(step):
-        return step + lax.div(step, 2) * (1 - 2 * lax.rem(step, 2))
-
-    def turn_of(step, on_core):
-        return order_of(step + on_core * (1 - 2 * lax.rem(step, 2)))
 
     children = [(c1, c2) for c1 in range(2) for c2 in range(2)]
 
@@ -477,11 +471,13 @@
                         obuf[step, i, x1, q1, 0, rows, :] = jnp.where(left_half, upper, pltpu.roll(lower, 64, 1))
                         obuf[step, i, x1, q1, 1, rows, :] = jnp.where(left_half, pltpu.roll(upper, 64, 1), lower)
 
-    def send_out(box, number):
-        i, hop, later = lax.rem(number, 2), lax.div(number, 2), lax.div(number, 8)
+    def send_out(half, number):
+        turn, round_ = lax.rem(number, 4), lax.div(number, 4)
+        box = 2 * half + lax.rem(lax.div(turn + 1, 2) + core, 2)
+        i = lax.rem(turn, 2)
         a1, a2 = box_of(box)
-        x = lax.rem(my_x + 1 + 2 * core + hop, 4)
-        c = lax.rem(later + core, 2)
+        x = lax.rem(my_x + 1 + 2 * core + round_ + turn, 4)
+        c = lax.rem(lax.div(round_, 4) + core, 2)
         to_bx, to_by = (2 * a1 + lax.rem(my_z + i, 2)) * 4 + x, 2 * (2 * a2 + core) + c
         src, dst = obuf.at[box, i, lax.div(x, 2), lax.rem(x, 2), c], orecv.at[chip]
         here = jnp.logical_and(to_bx == bx, to_by == by)
@@ -497,30 +493,19 @@
                 device_id=(to_bx, to_by), device_id_type=MESH,
             ).start()
 
-    def both(step, carry):
-        @pl.when(step < 4)
-        def _():
-            level1(order_of(step))
-
-        @pl.when(jnp.logical_and(step > 0, step < 5))
-        def _():
-            level23(turn_of(step - 1, core))
+    def two_boxes(half, carry):
+        for level in (level1, level23):
+            for box in range(2):
+                level(2 * half + box)
 
         def send_some(number, carry):
-            @pl.when(jnp.logical_and(step > 0, step < 5))
-            def _():
-                send_out(turn_of(step - 1, core), number)
-
-            @pl.when(step > 1)
-            def _():
-                send_out(turn_of(step - 2, core), number + 8)
-
+            send_out(half, number)
             return carry
 
-        lax.fori_loop(0, 8, send_some, 0)
-        return carry
-
-    lax.fori_loop(0, 6, both, 0)
+        lax.fori_loop(0, 32, send_some, 0)
+        return carry
+
+    lax.fori_loop(0, 2, two_boxes, 0)
 
     def settle(step, carry):
         pltpu.make_async_copy(zr.at[0], zr.at[0], sib_send.at[step]).wait()
@@ -538,9 +523,8 @@
             pltpu.make_async_copy(sbuf, sbuf, sem).wait()
 
     def arrive(step, carry):
-        box = turn_of(step, lax.rem(my_y, 2))
-        pltpu.make_async_copy(orecv.at[pl.ds(0, 16)], orecv.at[pl.ds(0, 16)], out_recv.at[box]).wait()
-        z1_from, y1_from = box_of(box)
+        pltpu.make_async_copy(orecv.at[pl.ds(0, 16)], orecv.at[pl.ds(0, 16)], out_recv.at[step]).wait()
+        z1_from, y1_from = box_of(step)
 
         def scatter_rows(i, carry):
             z, x, y = 2 * z1_from + lax.div(i, 8), lax.rem(lax.div(i, 2), 4), 2 * y1_from + lax.rem(i, 2)

time: 80.8 us -> 80 us (0.990)
  no operation moved by 1% of the time
where the time goes in v6:
time: 80 us; the launch traced here: 79.8 us
  Pallas kernels  78.4 us (98%)
  local copies, waits for them, and re-layouts  1.41 us (2%)
    pallas_call x1, Pallas kernels, shards(): pl.pallas_call(kernel, out_shape=jax.ShapeDtypeStruct((ROWS * 64, LANES),...  78.4 us

profile of v6, /device:TPU:1, one launch (start us, length us, event | category | flops | bytes accessed | tf_op | source)
XLA Modules:
  0.0 79.8 jit_solution(18311082908137562918)
XLA Ops:
  0.0 78.4 %shard_map.28 = f32[4608,128]{1,0:T(8,128)S(1)} custom-call(f32[4608,128]{1,0:T(8,128)} %bitcast.7, f32[4,96,96]{2,1,0:T(8,128)} %slow_hbm.1), custom_call_target="tpu_custom_call" | custom-call | tf_op jit(solution)/shard_map/pallas_call | solution.py:576
  78.4 1.4 %copy.4 = f32[2,6,64,6,128]{4,2,3,1,0:T(8,128)} copy(f32[2,6,64,6,128]{4,2,3,1,0:T(8,128)S(1)} %bitcast.6) | data formatting | bytes 4718592

commit v7 on v6

--- a/solution.py
+++ b/solution.py
@@ -140,7 +140,7 @@
 def kernel(
     coef_hbm, slow_hbm, out_ref,
     coef_ref, slow_ref, mix_ref, raw_ref,
-    sbuf, xin, s0, z1, zr, s2, obuf, orecv, vtab, e_tab, y_a, y_b, acc_a, acc_b,
+    sbuf, xin, s0, z1, zr, s2, obuf, orecv, vtab, e_tab, y_a, y_b, y_c, y_d, acc_a, acc_b,
     load, in_send, in_recv, sib_send, sib_recv, out_send, out_recv,
 ):
     bx, by = lax.axis_index("bx"), lax.axis_index("by")
@@ -337,6 +337,7 @@
         rows = pl.ds(pl.multiple_of(32 * q2, 8), 40)
         return jnp.concatenate([src[q1, rows, :], src[2 + q1, rows, :]], axis=0)
 
+    products = (y_a, y_b, y_c, y_d)
     pairs = ((0, y_a, acc_a), (1, y_b, acc_b))
 
     def x_of(slot):
@@ -384,25 +385,25 @@
             exponentials(24 + 2 * step + z0, (slot, slot + 2, slot, slot + 2), sizes)
         return carry
 
-    def level0(part, carry):
-        z0, y0 = lax.rem(my_z + lax.div(part, 2), 2), lax.rem(part, 2)
-        for slot, y_ref, _ in pairs:
+    def level0(half):
+        pltpu.make_async_copy(xin.at[0], xin.at[0], in_recv.at[half]).wait()
+        z0 = lax.rem(my_z + half, 2)
+        jobs = [(slot, y0, products[2 * y0 + slot]) for y0 in range(2) for slot in range(2)]
+        for slot, y0, y_ref in jobs:
             for c1, c2 in children:
                 z = 2 * c1 + z0
                 first = xin[slot, 0, z, 2 * c2 + y0]
                 second = permute(xin[slot, 1, z, 2 * c2 + 1 - y0], back)
                 interpolate(y_ref, 2 * c1 + c2, 2 * c1 + c2, [first, second])
-        for slot, y_ref, _ in pairs:
-            combine_cores(y_ref, (s0.at[slot, z0, y0, 0], s0.at[slot, z0, 1 - y0, 1]), 2 * part + slot)
-        return carry
+        for slot, y0, y_ref in jobs:
+            combine_cores(y_ref, (s0.at[slot, z0, y0, 0], s0.at[slot, z0, 1 - y0, 1]), 4 * half + 2 * y0 + slot)
 
     mixing_tables(mix_ref, raw_ref)
     for phases in (phases0, phases1, phases2):
         lax.fori_loop(0, 4, phases, 0)
 
     def arrived(half, carry):
-        pltpu.make_async_copy(xin.at[0], xin.at[0], in_recv.at[half]).wait()
-        lax.fori_loop(2 * half, 2 * half + 2, level0, 0)
+        level0(half)
 
         @pl.when(half == 0)
         def _():
@@ -412,45 +413,45 @@
 
     lax.fori_loop(0, 2, arrived, 0)
 
-    def level1(step):
-        a1, a2 = box_of(step)
-        for slot, y_ref, _ in pairs:
+    def level1(half):
+        jobs = [(2 * half + i, slot, products[2 * i + slot]) for i in range(2) for slot in range(2)]
+        for box, slot, y_ref in jobs:
+            a1, a2 = box_of(box)
             for c1, c2 in children:
                 blocks = [window(s0.at[slot, c1, c2, side], a1, a2) for side in range(2)]
                 interpolate(y_ref, 2 * c1 + c2, 4 + 4 * a2 + 2 * c1 + c2, blocks)
-        for slot, y_ref, _ in pairs:
+        for box, slot, y_ref in jobs:
             x1 = x_of(slot)[0]
-            combine_cores(y_ref, (z1.at[step, x1, 0], z1.at[step, x1, 1]), 8 + 2 * step + slot)
-        pltpu.make_async_remote_copy(
-            src_ref=z1.at[step, :, :, :, pl.ds(pl.multiple_of(32 * (1 - core), 8), 40), :],
-            dst_ref=zr.at[step],
-            send_sem=sib_send.at[step],
-            recv_sem=sib_recv.at[step],
-            device_id=(bx, my_y * 2 + 1 - core),
-            device_id_type=MESH,
-        ).start()
+            combine_cores(y_ref, (z1.at[box, x1, 0], z1.at[box, x1, 1]), 8 + 2 * box + slot)
+            if slot == 1:
+                pltpu.make_async_remote_copy(
+                    src_ref=z1.at[box, :, :, :, pl.ds(pl.multiple_of(32 * (1 - core), 8), 40), :],
+                    dst_ref=zr.at[box],
+                    send_sem=sib_send.at[box],
+                    recv_sem=sib_recv.at[box],
+                    device_id=(bx, my_y * 2 + 1 - core),
+                    device_id_type=MESH,
+                ).start()
 
     left = lax.broadcasted_iota(jnp.int32, (PAD, LANES), 1) < 64
     left_half = lax.broadcasted_iota(jnp.int32, (HALF, LANES), 1) < 64
 
-    def level23(step):
-        pltpu.make_async_copy(zr.at[0], zr.at[0], sib_recv.at[step]).wait()
-        near_z0 = lax.rem(my_z, 2)
-        z0_of = (near_z0, 1 - near_z0)
-        for i, y_ref, _ in pairs:
-            z0 = z0_of[i]
+    def level23(half, i):
+        z0 = lax.rem(my_z + i, 2)
+        jobs = [(2 * half + j, j, y_ref, acc_ref) for j, y_ref, acc_ref in pairs]
+        for box, j, y_ref, _ in jobs:
             for c1, c2 in children:
-                other = zr.at[step, c1, c2]
+                other = zr.at[box, c1, c2]
                 blocks = [
-                    window(z1.at[step, c1, c2], z0, core),
+                    window(z1.at[box, c1, c2], z0, core),
                     jnp.concatenate([other[z0], other[2 + z0]], axis=0),
                 ]
                 interpolate(y_ref, 2 * c1 + c2, 4 + 4 * core + 2 * c1 + c2, blocks)
-        for i, y_ref, _ in pairs:
-            combine_mirrored(y_ref, (s2.at[i, 0], s2.at[i, 1]), 16 + 2 * step + z0_of[i], back)
-        for i, y_ref, _ in pairs:
+        for box, j, y_ref, _ in jobs:
+            combine_mirrored(y_ref, (s2.at[j, 0], s2.at[j, 1]), 16 + 2 * box + z0, back)
+        for box, j, y_ref, _ in jobs:
             for c1 in range(2):
-                src = s2.at[i, lax.rem(c1 + core, 2)]
+                src = s2.at[j, lax.rem(c1 + core, 2)]
                 near, far = [], []
                 for x1 in range(2):
                     first = window(src, x1, 0)
@@ -460,23 +461,22 @@
                     far.append(jnp.where(left, permute(first, back), permute(second, back_half)))
                 interpolate(y_ref, 2 * c1, 4 + 2 * c1, near)
                 interpolate(y_ref, 2 * c1 + 1, 4 + 2 * c1 + 1, far)
-        for i, y_ref, acc_ref in pairs:
-            combine_mirrored(y_ref, (acc_ref.at[0], acc_ref.at[1]), 24 + 2 * step + z0_of[i], back_half)
+        for box, j, y_ref, acc_ref in jobs:
+            combine_mirrored(y_ref, (acc_ref.at[0], acc_ref.at[1]), 24 + 2 * box + z0, back_half)
             for x1 in range(2):
                 for q1 in range(2):
                     for part in range(2):
                         upper = acc_ref[x1, 2 * part + q1, 0:HALF, :]
                         lower = acc_ref[x1, 2 * part + q1, HALF:ROWS, :]
                         rows = pl.ds(HALF * part, HALF)
-                        obuf[step, i, x1, q1, 0, rows, :] = jnp.where(left_half, upper, pltpu.roll(lower, 64, 1))
-                        obuf[step, i, x1, q1, 1, rows, :] = jnp.where(left_half, pltpu.roll(upper, 64, 1), lower)
-
-    def send_out(half, number):
-        turn, round_ = lax.rem(number, 4), lax.div(number, 4)
-        box = 2 * half + lax.rem(lax.div(turn + 1, 2) + core, 2)
-        i = lax.rem(turn, 2)
+                        obuf[box, i, x1, q1, 0, rows, :] = jnp.where(left_half, upper, pltpu.roll(lower, 64, 1))
+                        obuf[box, i, x1, q1, 1, rows, :] = jnp.where(left_half, pltpu.roll(upper, 64, 1), lower)
+
+    def send_out(half, i, number):
+        turn, round_ = lax.rem(number, 2), lax.div(number, 2)
+        box = 2 * half + lax.rem(turn + core, 2)
         a1, a2 = box_of(box)
-        x = lax.rem(my_x + 1 + 2 * core + round_ + turn, 4)
+        x = lax.rem(my_x + 1 + 2 * core + round_ + 2 * turn, 4)
         c = lax.rem(lax.div(round_, 4) + core, 2)
         to_bx, to_by = (2 * a1 + lax.rem(my_z + i, 2)) * 4 + x, 2 * (2 * a2 + core) + c
         src, dst = obuf.at[box, i, lax.div(x, 2), lax.rem(x, 2), c], orecv.at[chip]
@@ -494,15 +494,21 @@
             ).start()
 
     def two_boxes(half, carry):
-        for level in (level1, level23):
-            for box in range(2):
-                level(2 * half + box)
-
-        def send_some(number, carry):
-            send_out(half, number)
+        level1(half)
+        for box in range(2):
+            pltpu.make_async_copy(zr.at[0], zr.at[0], sib_recv.at[2 * half + box]).wait()
+
+        def both_z(i, carry):
+            level23(half, i)
+
+            def send_some(number, carry):
+                send_out(half, i, number)
+                return carry
+
+            lax.fori_loop(0, 16, send_some, 0)
             return carry
 
-        lax.fori_loop(0, 32, send_some, 0)
+        lax.fori_loop(0, 2, both_z, 0)
         return carry
 
     lax.fori_loop(0, 2, two_boxes, 0)
@@ -558,6 +564,8 @@
             (64,) + dense,
             (29, TERMS, LANES),
             (32, 4, 2, TERMS, LANES),
+            (4, 2 * TERMS, 2 * LANES),
+            (4, 2 * TERMS, 2 * LANES),
             (4, 2 * TERMS, 2 * LANES),
             (4, 2 * TERMS, 2 * LANES),
             (2, 4) + dense,

time: 80 us -> 78.6 us (0.982)
  Pallas kernels: 78.4 us -> 77.1 us
    pallas_call x1, Pallas kernels: 78.4 us -> 77.1 us  [shards(): pl.pallas_call(kernel, out_shape=jax.ShapeDtypeStruct((ROWS * 64, LANES),...]
where the time goes in v7:
time: 78.6 us; the launch traced here: 78.5 us
  Pallas kernels  77.1 us (98%)
  local copies, waits for them, and re-layouts  1.41 us (2%)
    pallas_call x1, Pallas kernels, shards(): pl.pallas_call(kernel, out_shape=jax.ShapeDtypeStruct((ROWS * 64, LANES),...  77.1 us

profile of v7, /device:TPU:1, one launch (start us, length us, event | category | flops | bytes accessed | tf_op | source)
XLA Modules:
  0.0 78.5 jit_solution(9063172728888901492)
XLA Ops:
  0.0 77.1 %shard_map.28 = f32[4608,128]{1,0:T(8,128)S(1)} custom-call(f32[4608,128]{1,0:T(8,128)} %bitcast.7, f32[4,96,96]{2,1,0:T(8,128)} %slow_hbm.1), custom_call_target="tpu_custom_call" | custom-call | tf_op jit(solution)/shard_map/pallas_call | solution.py:584
  77.1 1.4 %copy.4 = f32[2,6,64,6,128]{4,2,3,1,0:T(8,128)} copy(f32[2,6,64,6,128]{4,2,3,1,0:T(8,128)S(1)} %bitcast.6) | data formatting | bytes 4718592

commit v8 on v7

--- a/solution.py
+++ b/solution.py
@@ -140,7 +140,7 @@
 def kernel(
     coef_hbm, slow_hbm, out_ref,
     coef_ref, slow_ref, mix_ref, raw_ref,
-    sbuf, xin, s0, z1, zr, s2, obuf, orecv, vtab, e_tab, y_a, y_b, y_c, y_d, acc_a, acc_b,
+    sbuf, xin, s0, z1, zr, s2, obuf, orecv, vtab, e_tab, y_a, y_b, acc_a, acc_b,
     load, in_send, in_recv, sib_send, sib_recv, out_send, out_recv,
 ):
     bx, by = lax.axis_index("bx"), lax.axis_index("by")
@@ -180,26 +180,26 @@
     pl.semaphore_wait(barrier, 127)
 
     def send_in(step, carry):
-        half, inner = lax.div(step, 32), lax.rem(step, 32)
-        dx, group = lax.rem(inner, 4), lax.div(inner, 4)
-        dy = lax.rem(dx + group, 4)
-        dz = half + 2 * lax.rem(lax.div(group, 4) + dx, 2)
-        dx, dz, dy = [lax.rem(d + 2 * core, 4) for d in (dx, dz, dy)]
+        half, part, inner = lax.div(step, 32), lax.div(step, 16), lax.rem(step, 16)
+        even, far_z = lax.rem(inner + core, 2), lax.rem(lax.div(inner, 2), 2)
+        dx = (1 - even) * (2 * half + 1) + even * 2 * lax.rem(half + my_x0, 2)
+        dy = lax.rem(lax.div(inner, 4) + lax.rem(inner, 2) + 2 * far_z + 2 * core, 4)
+        dz = lax.rem(lax.rem(part, 2) + 2 * far_z + 2 * core, 4)
         to_x, to_z, to_y = lax.rem(my_x + dx, 4), lax.rem(my_z + dz, 4), lax.rem(my_y + dy, 4)
         to_bx, to_by = to_z * 4 + to_x, to_y * 2 + my_x0
         ell = to_z * 16 + to_x * 4 + to_y
         src = sbuf.at[ell]
-        dst = xin.at[lax.div(dx, 2), core, my_z, my_y]
+        dst = xin.at[half, core, my_z, my_y]
         here = jnp.logical_and(to_bx == bx, to_by == by)
 
         @pl.when(here)
         def _():
-            pltpu.make_async_copy(src, dst, in_recv.at[half]).start()
+            pltpu.make_async_copy(src, dst, in_recv.at[part]).start()
 
         @pl.when(jnp.logical_not(here))
         def _():
             pltpu.make_async_remote_copy(
-                src_ref=src, dst_ref=dst, send_sem=in_send, recv_sem=in_recv.at[half],
+                src_ref=src, dst_ref=dst, send_sem=in_send, recv_sem=in_recv.at[part],
                 device_id=(to_bx, to_by), device_id_type=MESH,
             ).start()
 
@@ -337,11 +337,11 @@
         rows = pl.ds(pl.multiple_of(32 * q2, 8), 40)
         return jnp.concatenate([src[q1, rows, :], src[2 + q1, rows, :]], axis=0)
 
-    products = (y_a, y_b, y_c, y_d)
     pairs = ((0, y_a, acc_a), (1, y_b, acc_b))
 
     def x_of(slot):
-        dx = 2 * slot + lax.rem(my_x + core, 2)
+        odd = lax.rem(my_x + core, 2)
+        dx = odd * (2 * slot + 1) + (1 - odd) * 2 * lax.rem(slot + core, 2)
         x = lax.rem(my_x - dx + 4, 4)
         return lax.div(x, 2), low1 + 4 * lax.div(x, 2) + 8 * core
 
@@ -353,11 +353,11 @@
     children = [(c1, c2) for c1 in range(2) for c2 in range(2)]
 
     def phases0(part, carry):
-        z0, y0 = lax.rem(my_z + lax.div(part, 2), 2), lax.rem(part, 2)
-        for slot in range(2):
-            r1 = x_of(slot)[1] + 2 * z0
+        z0 = lax.rem(my_z + part, 2)
+        r1 = x_of(lax.div(part, 2))[1] + 2 * z0
+        for y0 in range(2):
             sizes = [magnitude(0, r1 + c1, c1, lane2 + (c2 + 2 * y0), c2) for c1, c2 in children]
-            exponentials(2 * part + slot, (0,) * 4, sizes)
+            exponentials(2 * part + y0, (0,) * 4, sizes)
         return carry
 
     def phases1(step, carry):
@@ -385,53 +385,49 @@
             exponentials(24 + 2 * step + z0, (slot, slot + 2, slot, slot + 2), sizes)
         return carry
 
-    def level0(half):
-        pltpu.make_async_copy(xin.at[0], xin.at[0], in_recv.at[half]).wait()
-        z0 = lax.rem(my_z + half, 2)
-        jobs = [(slot, y0, products[2 * y0 + slot]) for y0 in range(2) for slot in range(2)]
-        for slot, y0, y_ref in jobs:
+    def level0(part, carry):
+        pltpu.make_async_copy(xin.at[0, 0], xin.at[0, 0], in_recv.at[part]).wait()
+        slot, z0 = lax.div(part, 2), lax.rem(my_z + part, 2)
+        for y0, y_ref, _ in pairs:
             for c1, c2 in children:
                 z = 2 * c1 + z0
                 first = xin[slot, 0, z, 2 * c2 + y0]
                 second = permute(xin[slot, 1, z, 2 * c2 + 1 - y0], back)
                 interpolate(y_ref, 2 * c1 + c2, 2 * c1 + c2, [first, second])
-        for slot, y0, y_ref in jobs:
-            combine_cores(y_ref, (s0.at[slot, z0, y0, 0], s0.at[slot, z0, 1 - y0, 1]), 4 * half + 2 * y0 + slot)
-
-    mixing_tables(mix_ref, raw_ref)
-    for phases in (phases0, phases1, phases2):
-        lax.fori_loop(0, 4, phases, 0)
-
-    def arrived(half, carry):
-        level0(half)
-
-        @pl.when(half == 0)
-        def _():
-            lax.fori_loop(0, 4, phases3, 0)
-
-        return carry
-
-    lax.fori_loop(0, 2, arrived, 0)
-
-    def level1(half):
-        jobs = [(2 * half + i, slot, products[2 * i + slot]) for i in range(2) for slot in range(2)]
-        for box, slot, y_ref in jobs:
-            a1, a2 = box_of(box)
+        for y0, y_ref, _ in pairs:
+            combine_cores(y_ref, (s0.at[slot, z0, y0, 0], s0.at[slot, z0, 1 - y0, 1]), 2 * part + y0)
+        return carry
+
+    def level1(half, slot):
+        x1 = x_of(slot)[0]
+        for i, y_ref, _ in pairs:
+            a1, a2 = box_of(2 * half + i)
             for c1, c2 in children:
                 blocks = [window(s0.at[slot, c1, c2, side], a1, a2) for side in range(2)]
                 interpolate(y_ref, 2 * c1 + c2, 4 + 4 * a2 + 2 * c1 + c2, blocks)
-        for box, slot, y_ref in jobs:
-            x1 = x_of(slot)[0]
+        for i, y_ref, _ in pairs:
+            box = 2 * half + i
             combine_cores(y_ref, (z1.at[box, x1, 0], z1.at[box, x1, 1]), 8 + 2 * box + slot)
-            if slot == 1:
-                pltpu.make_async_remote_copy(
-                    src_ref=z1.at[box, :, :, :, pl.ds(pl.multiple_of(32 * (1 - core), 8), 40), :],
-                    dst_ref=zr.at[box],
-                    send_sem=sib_send.at[box],
-                    recv_sem=sib_recv.at[box],
-                    device_id=(bx, my_y * 2 + 1 - core),
-                    device_id_type=MESH,
-                ).start()
+            pltpu.make_async_remote_copy(
+                src_ref=z1.at[box, x1, :, :, pl.ds(pl.multiple_of(32 * (1 - core), 8), 40), :],
+                dst_ref=zr.at[box, x1],
+                send_sem=sib_send.at[box],
+                recv_sem=sib_recv.at[box],
+                device_id=(bx, my_y * 2 + 1 - core),
+                device_id_type=MESH,
+            ).start()
+
+    mixing_tables(mix_ref, raw_ref)
+    for phases, boxes in ((phases0, 4), (phases1, 4), (phases2, 2), (phases3, 2)):
+        lax.fori_loop(0, boxes, phases, 0)
+
+    def first_slot(half, carry):
+        level1(half, 0)
+        return carry
+
+    lax.fori_loop(0, 2, level0, 0)
+    lax.fori_loop(0, 2, first_slot, 0)
+    lax.fori_loop(2, 4, level0, 0)
 
     left = lax.broadcasted_iota(jnp.int32, (PAD, LANES), 1) < 64
     left_half = lax.broadcasted_iota(jnp.int32, (HALF, LANES), 1) < 64
@@ -494,7 +490,7 @@
             ).start()
 
     def two_boxes(half, carry):
-        level1(half)
+        level1(half, 1)
         for box in range(2):
             pltpu.make_async_copy(zr.at[0], zr.at[0], sib_recv.at[2 * half + box]).wait()
 
@@ -509,6 +505,12 @@
             return carry
 
         lax.fori_loop(0, 2, both_z, 0)
+
+        @pl.when(half == 0)
+        def _():
+            for phases in (phases2, phases3):
+                lax.fori_loop(2, 4, phases, 0)
+
         return carry
 
     lax.fori_loop(0, 2, two_boxes, 0)
@@ -566,8 +568,6 @@
             (32, 4, 2, TERMS, LANES),
             (4, 2 * TERMS, 2 * LANES),
             (4, 2 * TERMS, 2 * LANES),
-            (4, 2 * TERMS, 2 * LANES),
-            (4, 2 * TERMS, 2 * LANES),
             (2, 4) + dense,
             (2, 4) + dense,
         )
@@ -575,7 +575,7 @@
     scratch += [
         pltpu.SemaphoreType.DMA((4,)),
         pltpu.SemaphoreType.DMA,
-        pltpu.SemaphoreType.DMA((2,)),
+        pltpu.SemaphoreType.DMA((4,)),
         pltpu.SemaphoreType.DMA((4,)),
         pltpu.SemaphoreType.DMA((4,)),
         pltpu.SemaphoreType.DMA,

time: 78.6 us -> 77.8 us (0.990)
  Pallas kernels: 77.1 us -> 76.2 us
    pallas_call x1, Pallas kernels: 77.1 us -> 76.2 us  [shards(): pl.pallas_call(kernel, out_shape=jax.ShapeDtypeStruct((ROWS * 64, LANES),...]
where the time goes in v8:
time: 77.8 us; the launch traced here: 77.7 us
  Pallas kernels  76.2 us (98%)
  local copies, waits for them, and re-layouts  1.41 us (2%)
    pallas_call x1, Pallas kernels, shards(): pl.pallas_call(kernel, out_shape=jax.ShapeDtypeStruct((ROWS * 64, LANES),...  76.2 us

profile of v8, /device:TPU:1, one launch (start us, length us, event | category | flops | bytes accessed | tf_op | source)
XLA Modules:
  0.0 77.7 jit_solution(11478448133100716137)
XLA Ops:
  0.0 76.2 %shard_map.28 = f32[4608,128]{1,0:T(8,128)S(1)} custom-call(f32[4608,128]{1,0:T(8,128)} %bitcast.7, f32[4,96,96]{2,1,0:T(8,128)} %slow_hbm.1), custom_call_target="tpu_custom_call" | custom-call | tf_op jit(solution)/shard_map/pallas_call | solution.py:584
  76.3 1.4 %copy.4 = f32[2,6,64,6,128]{4,2,3,1,0:T(8,128)} copy(f32[2,6,64,6,128]{4,2,3,1,0:T(8,128)S(1)} %bitcast.6) | data formatting | bytes 4718592

commit v9 on v8

--- a/solution.py
+++ b/solution.py
@@ -150,12 +150,9 @@
     chip = bx * 4 + my_y
     low1 = reverse6(chip) * 16
 
-    loads = [
-        pltpu.make_async_copy(src, dst, load.at[i])
-        for i, (src, dst) in enumerate(
-            ((coef_hbm, coef_ref), (slow_hbm, slow_ref))
-        )
-    ]
+    chunks = [coef_ref.at[pl.ds(1536 * i, 1536)] for i in range(3)]
+    loads = [pltpu.make_async_copy(coef_hbm.at[pl.ds(1536 * i, 1536)], chunks[i], load.at[i]) for i in range(3)]
+    loads.append(pltpu.make_async_copy(slow_hbm, slow_ref, load.at[3]))
     for copy in loads:
         copy.start()
 
@@ -169,27 +166,26 @@
 
     lax.fori_loop(1, 121, greet, 0, unroll=8)
     lax.fori_loop(121, 128, greet, 0, unroll=7)
-    loads[0].wait()
-
-    def gather_rows(ell, carry):
-        for tile in range(9):
-            sbuf[ell, 8 * tile : 8 * tile + 8, :] = coef_ref[pl.ds(tile * 512 + ell, 8, stride=64), :]
-        return carry
-
-    lax.fori_loop(0, 64, gather_rows, 0, unroll=8)
-    pl.semaphore_wait(barrier, 127)
-
-    def send_in(step, carry):
+    def target_in(step):
         half, part, inner = lax.div(step, 32), lax.div(step, 16), lax.rem(step, 16)
         even, far_z = lax.rem(inner + core, 2), lax.rem(lax.div(inner, 2), 2)
         dx = (1 - even) * (2 * half + 1) + even * 2 * lax.rem(half + my_x0, 2)
         dy = lax.rem(lax.div(inner, 4) + lax.rem(inner, 2) + 2 * far_z + 2 * core, 4)
         dz = lax.rem(lax.rem(part, 2) + 2 * far_z + 2 * core, 4)
-        to_x, to_z, to_y = lax.rem(my_x + dx, 4), lax.rem(my_z + dz, 4), lax.rem(my_y + dy, 4)
+        return lax.rem(my_z + dz, 4), lax.rem(my_x + dx, 4), lax.rem(my_y + dy, 4)
+
+    def gather_rows(step, carry):
+        z, x, y = target_in(step)
+        ell = z * 16 + x * 4 + y
+        for tile in range(9):
+            sbuf[ell, 8 * tile : 8 * tile + 8, :] = coef_ref[pl.ds(tile * 512 + ell, 8, stride=64), :]
+        return carry
+
+    def send_in(step, carry):
+        half, part = lax.div(step, 32), lax.div(step, 16)
+        to_z, to_x, to_y = target_in(step)
         to_bx, to_by = to_z * 4 + to_x, to_y * 2 + my_x0
-        ell = to_z * 16 + to_x * 4 + to_y
-        src = sbuf.at[ell]
-        dst = xin.at[half, core, my_z, my_y]
+        src, dst = sbuf.at[to_z * 16 + to_x * 4 + to_y], xin.at[half, core, my_z, my_y]
         here = jnp.logical_and(to_bx == bx, to_by == by)
 
         @pl.when(here)
@@ -205,9 +201,18 @@
 
         return carry
 
-    lax.fori_loop(0, 64, send_in, 0)
-
-    loads[1].wait()
+    def send_and_gather(step, carry):
+        send_in(step, carry)
+        return gather_rows(step + 16, carry)
+
+    for copy in loads[:3]:
+        copy.wait()
+    lax.fori_loop(0, 16, gather_rows, 0, unroll=4)
+    pl.semaphore_wait(barrier, 127)
+    lax.fori_loop(0, 48, send_and_gather, 0)
+    lax.fori_loop(48, 64, send_in, 0)
+
+    loads[3].wait()
     lane = lax.broadcasted_iota(jnp.int32, (TERMS, 96), 1).astype(jnp.float32)
     row = lax.broadcasted_iota(jnp.int32, (TERMS, 96), 0).astype(jnp.float32)
     q1, q2, t1, t2 = digits(row, 2, 2, CHEB, CHEB)
@@ -473,19 +478,19 @@
         box = 2 * half + lax.rem(turn + core, 2)
         a1, a2 = box_of(box)
         x = lax.rem(my_x + 1 + 2 * core + round_ + 2 * turn, 4)
-        c = lax.rem(lax.div(round_, 4) + core, 2)
+        c = lax.rem(round_ + lax.div(round_, 4) + turn, 2)
         to_bx, to_by = (2 * a1 + lax.rem(my_z + i, 2)) * 4 + x, 2 * (2 * a2 + core) + c
         src, dst = obuf.at[box, i, lax.div(x, 2), lax.rem(x, 2), c], orecv.at[chip]
         here = jnp.logical_and(to_bx == bx, to_by == by)
 
         @pl.when(here)
         def _():
-            pltpu.make_async_copy(src, dst, out_recv.at[box]).start()
+            pltpu.make_async_copy(src, dst, out_recv.at[2 * half + i]).start()
 
         @pl.when(jnp.logical_not(here))
         def _():
             pltpu.make_async_remote_copy(
-                src_ref=src, dst_ref=dst, send_sem=out_send, recv_sem=out_recv.at[box],
+                src_ref=src, dst_ref=dst, send_sem=out_send, recv_sem=out_recv.at[2 * half + i],
                 device_id=(to_bx, to_by), device_id_type=MESH,
             ).start()
 
@@ -532,10 +537,13 @@
 
     def arrive(step, carry):
         pltpu.make_async_copy(orecv.at[pl.ds(0, 16)], orecv.at[pl.ds(0, 16)], out_recv.at[step]).wait()
-        z1_from, y1_from = box_of(step)
 
         def scatter_rows(i, carry):
-            z, x, y = 2 * z1_from + lax.div(i, 8), lax.rem(lax.div(i, 2), 4), 2 * y1_from + lax.rem(i, 2)
+            upper = lax.div(i, 8)
+            z = 2 * upper + lax.rem(my_z + step, 2)
+            other = lax.rem(lax.div(my_z, 2) + upper + lax.div(step, 2), 2)
+            y = 2 * lax.rem(lax.div(my_y, 2) + other, 2) + lax.rem(i, 2)
+            x = lax.rem(lax.div(i, 2), 4)
             ell = z * 16 + x * 4 + y
             for tile in range(9):
                 out_ref[pl.ds(tile * 512 + ell, 8, stride=64), :] = orecv[ell, 8 * tile : 8 * tile + 8, :]

time: 77.8 us -> 76.7 us (0.986)
  Pallas kernels: 76.2 us -> 75.2 us
    pallas_call x1, Pallas kernels: 76.2 us -> 75.2 us  [shards(): pl.pallas_call(kernel, out_shape=jax.ShapeDtypeStruct((ROWS * 64, LANES),...]
where the time goes in v9:
time: 76.7 us; the launch traced here: 76.6 us
  Pallas kernels  75.2 us (98%)
  local copies, waits for them, and re-layouts  1.41 us (2%)
    pallas_call x1, Pallas kernels, shards(): pl.pallas_call(kernel, out_shape=jax.ShapeDtypeStruct((ROWS * 64, LANES),...  75.2 us

profile of v9, /device:TPU:1, one launch (start us, length us, event | category | flops | bytes accessed | tf_op | source)
XLA Modules:
  0.0 76.6 jit_solution(12526608484514082932)
XLA Ops:
  0.0 75.2 %shard_map.28 = f32[4608,128]{1,0:T(8,128)S(1)} custom-call(f32[4608,128]{1,0:T(8,128)} %bitcast.7, f32[4,96,96]{2,1,0:T(8,128)} %slow_hbm.1), custom_call_target="tpu_custom_call" | custom-call | tf_op jit(solution)/shard_map/pallas_call | solution.py:592
  75.2 1.4 %copy.4 = f32[2,6,64,6,128]{4,2,3,1,0:T(8,128)} copy(f32[2,6,64,6,128]{4,2,3,1,0:T(8,128)S(1)} %bitcast.6) | data formatting | bytes 4718592

commit v10 on v9

--- a/solution.py
+++ b/solution.py
@@ -139,7 +139,7 @@
 
 def kernel(
     coef_hbm, slow_hbm, out_ref,
-    coef_ref, slow_ref, mix_ref, raw_ref,
+    coef_ref, slow_ref, mix_ref, raw_ref, pieces_ref,
     sbuf, xin, s0, z1, zr, s2, obuf, orecv, vtab, e_tab, y_a, y_b, acc_a, acc_b,
     load, in_send, in_recv, sib_send, sib_recv, out_send, out_recv,
 ):
@@ -157,70 +157,86 @@
         copy.start()
 
     barrier = pltpu.get_barrier_semaphore()
-    me = bx * 8 + by
+    across = [lax.rem(by + j, 8) for j in range(8)]
 
     def greet(i, carry):
-        there = lax.rem(me + i, 128)
-        pl.semaphore_signal(barrier, inc=1, device_id=(lax.div(there, 8), lax.rem(there, 8)), device_id_type=MESH)
-        return carry
-
-    lax.fori_loop(1, 121, greet, 0, unroll=8)
-    lax.fori_loop(121, 128, greet, 0, unroll=7)
-    def target_in(step):
-        half, part, inner = lax.div(step, 32), lax.div(step, 16), lax.rem(step, 16)
-        even, far_z = lax.rem(inner + core, 2), lax.rem(lax.div(inner, 2), 2)
-        dx = (1 - even) * (2 * half + 1) + even * 2 * lax.rem(half + my_x0, 2)
-        dy = lax.rem(lax.div(inner, 4) + lax.rem(inner, 2) + 2 * far_z + 2 * core, 4)
-        dz = lax.rem(lax.rem(part, 2) + 2 * far_z + 2 * core, 4)
-        return lax.rem(my_z + dz, 4), lax.rem(my_x + dx, 4), lax.rem(my_y + dy, 4)
-
-    def gather_rows(step, carry):
-        z, x, y = target_in(step)
+        there = lax.rem(bx + i, 16)
+        for j in range(8):
+
+            @pl.when(i + j > 0)
+            def _(j=j):
+                pl.semaphore_signal(barrier, inc=1, device_id=(there, across[j]), device_id_type=MESH)
+
+        return carry
+
+    lax.fori_loop(0, 16, greet, 0)
+
+    y_at = [lax.rem(my_y + 2 * core + v, 4) for v in range(4)]
+
+    def targets_in(part):
+        half = lax.div(part, 2)
+        odd = lax.rem(my_x + 2 * half + 1, 4)
+        even = lax.rem(my_x + 2 * lax.rem(half + my_x0, 2), 4)
+        x_at = (odd + core * (even - odd), even + core * (odd - even))
+        z_at = [lax.rem(my_z + lax.rem(part, 2) + 2 * far + 2 * core, 4) for far in range(2)]
+        for inner in range(16):
+            far = inner // 2 % 2
+            yield z_at[far], x_at[inner % 2], y_at[(inner // 4 + inner % 2 + 2 * far) % 4]
+
+    def gather_rows(z, x, y):
         ell = z * 16 + x * 4 + y
         for tile in range(9):
             sbuf[ell, 8 * tile : 8 * tile + 8, :] = coef_ref[pl.ds(tile * 512 + ell, 8, stride=64), :]
-        return carry
-
-    def send_in(step, carry):
-        half, part = lax.div(step, 32), lax.div(step, 16)
-        to_z, to_x, to_y = target_in(step)
-        to_bx, to_by = to_z * 4 + to_x, to_y * 2 + my_x0
-        src, dst = sbuf.at[to_z * 16 + to_x * 4 + to_y], xin.at[half, core, my_z, my_y]
-        here = jnp.logical_and(to_bx == bx, to_by == by)
-
-        @pl.when(here)
+
+    def send_part(part, carry):
+        half = lax.div(part, 2)
+        for z, x, y in targets_in(part):
+            to_bx, to_by = z * 4 + x, y * 2 + my_x0
+            src, dst = sbuf.at[z * 16 + x * 4 + y], xin.at[half, core, my_z, my_y]
+            here = jnp.logical_and(to_bx == bx, to_by == by)
+
+            @pl.when(here)
+            def _(src=src, dst=dst):
+                pltpu.make_async_copy(src, dst, in_recv.at[part]).start()
+
+            @pl.when(jnp.logical_not(here))
+            def _(src=src, dst=dst, to_bx=to_bx, to_by=to_by):
+                pltpu.make_async_remote_copy(
+                    src_ref=src, dst_ref=dst, send_sem=in_send, recv_sem=in_recv.at[part],
+                    device_id=(to_bx, to_by), device_id_type=MESH,
+                ).start()
+
+        @pl.when(part < 3)
         def _():
-            pltpu.make_async_copy(src, dst, in_recv.at[part]).start()
-
-        @pl.when(jnp.logical_not(here))
-        def _():
-            pltpu.make_async_remote_copy(
-                src_ref=src, dst_ref=dst, send_sem=in_send, recv_sem=in_recv.at[part],
-                device_id=(to_bx, to_by), device_id_type=MESH,
-            ).start()
-
-        return carry
-
-    def send_and_gather(step, carry):
-        send_in(step, carry)
-        return gather_rows(step + 16, carry)
+            for target in targets_in(part + 1):
+                gather_rows(*target)
+
+        return carry
 
     for copy in loads[:3]:
         copy.wait()
-    lax.fori_loop(0, 16, gather_rows, 0, unroll=4)
+    for target in targets_in(jnp.int32(0)):
+        gather_rows(*target)
     pl.semaphore_wait(barrier, 127)
-    lax.fori_loop(0, 48, send_and_gather, 0)
-    lax.fori_loop(48, 64, send_in, 0)
+    lax.fori_loop(0, 4, send_part, 0)
 
     loads[3].wait()
-    lane = lax.broadcasted_iota(jnp.int32, (TERMS, 96), 1).astype(jnp.float32)
-    row = lax.broadcasted_iota(jnp.int32, (TERMS, 96), 0).astype(jnp.float32)
+    for level in range(4):
+        table = jnp.concatenate([slow_ref[level], jnp.zeros((96, LANES - 96), jnp.float32)], axis=1)
+        for piece in range(3):
+            rounded = table.astype(jnp.bfloat16)
+            pieces_ref[level, :, piece * LANES : piece * LANES + LANES] = rounded
+            table = table - rounded.astype(jnp.float32)
+    lane = lax.broadcasted_iota(jnp.int32, (TERMS, LANES), 1).astype(jnp.float32)
+    row = lax.broadcasted_iota(jnp.int32, (TERMS, LANES), 0).astype(jnp.float32)
     q1, q2, t1, t2 = digits(row, 2, 2, CHEB, CHEB)
     row_i, row_j = CHEB * q1 + t1, CHEB * q2 + t2
+    left_rows = lane < 64
 
     def spread(level, a1):
-        pick = jnp.where(row_i + (12 * a1).astype(jnp.float32) == lane, 1.0, 0.0)
-        return jnp.dot(pick, slow_ref[level], precision=lax.Precision.HIGHEST, preferred_element_type=jnp.float32)
+        pick = jnp.where(row_i[:, 0:96] + (12 * a1).astype(jnp.float32) == lane[:, 0:96], 1.0, 0.0)
+        found = jnp.dot(pick.astype(jnp.bfloat16), pieces_ref[level], preferred_element_type=jnp.float32)
+        return found[:, 0:LANES] + found[:, LANES : 2 * LANES] + found[:, 2 * LANES :]
 
     def column(table, a2):
         picked = jnp.where(row_j + (12 * a2).astype(jnp.float32) == lane, table, 0.0)
@@ -237,23 +253,20 @@
 
     lax.fori_loop(0, 2, fill1, 0)
 
-    def fill2(z, carry):
-        table = spread(2, z)
-        for a2 in range(2):
-            vtab[5 + 2 * z + a2] = column(table, 2 * a2 + core)
-        return carry
-
-    lax.fori_loop(0, 4, fill2, 0)
-    left_rows = lax.broadcasted_iota(jnp.int32, (TERMS, LANES), 1) < 64
-
-    def fill3(a1, carry):
-        table = spread(3, a1)
-        for a2 in range(2):
-            box = 2 * (2 * a2 + core)
-            vtab[13 + 2 * a1 + a2] = jnp.where(left_rows, column(table, box), column(table, box + 1))
-        return carry
-
-    lax.fori_loop(0, 8, fill3, 0)
+    def fill23(half):
+        def fill(z, carry):
+            other = lax.rem(lax.div(z, 2) + lax.div(my_z, 2) + half, 2)
+            a2 = lax.rem(lax.div(my_y, 2) + other, 2)
+            box = 2 * a2 + core
+            vtab[5 + 2 * z + a2] = column(spread(2, z), box)
+            for x1 in range(2):
+                table = spread(3, 2 * z + x1)
+                vtab[13 + 4 * z + 2 * x1 + a2] = jnp.where(left_rows, column(table, 2 * box), column(table, 2 * box + 1))
+            return carry
+
+        lax.fori_loop(0, 4, fill, 0)
+
+    fill23(0)
 
     lanes = lax.broadcasted_iota(jnp.int32, (8, LANES), 1)
     low2 = reverse6(lax.rem(lanes, 64)) * 16
@@ -470,29 +483,33 @@
                         upper = acc_ref[x1, 2 * part + q1, 0:HALF, :]
                         lower = acc_ref[x1, 2 * part + q1, HALF:ROWS, :]
                         rows = pl.ds(HALF * part, HALF)
-                        obuf[box, i, x1, q1, 0, rows, :] = jnp.where(left_half, upper, pltpu.roll(lower, 64, 1))
-                        obuf[box, i, x1, q1, 1, rows, :] = jnp.where(left_half, pltpu.roll(upper, 64, 1), lower)
-
-    def send_out(half, i, number):
-        turn, round_ = lax.rem(number, 2), lax.div(number, 2)
-        box = 2 * half + lax.rem(turn + core, 2)
-        a1, a2 = box_of(box)
-        x = lax.rem(my_x + 1 + 2 * core + round_ + 2 * turn, 4)
-        c = lax.rem(round_ + lax.div(round_, 4) + turn, 2)
-        to_bx, to_by = (2 * a1 + lax.rem(my_z + i, 2)) * 4 + x, 2 * (2 * a2 + core) + c
-        src, dst = obuf.at[box, i, lax.div(x, 2), lax.rem(x, 2), c], orecv.at[chip]
-        here = jnp.logical_and(to_bx == bx, to_by == by)
-
-        @pl.when(here)
-        def _():
-            pltpu.make_async_copy(src, dst, out_recv.at[2 * half + i]).start()
-
-        @pl.when(jnp.logical_not(here))
-        def _():
-            pltpu.make_async_remote_copy(
-                src_ref=src, dst_ref=dst, send_sem=out_send, recv_sem=out_recv.at[2 * half + i],
-                device_id=(to_bx, to_by), device_id_type=MESH,
-            ).start()
+                        obuf[box, i, 2 * x1 + q1, 0, rows, :] = jnp.where(left_half, upper, pltpu.roll(lower, 64, 1))
+                        obuf[box, i, 2 * x1 + q1, 1, rows, :] = jnp.where(left_half, pltpu.roll(upper, 64, 1), lower)
+
+    x_out = [lax.rem(my_x + 1 + 2 * core + k, 4) for k in range(4)]
+
+    def send_out(half, i):
+        boxes = [2 * half + core, 2 * half + 1 - core]
+        z0 = lax.rem(my_z + i, 2)
+        places = [box_of(box) for box in boxes]
+        places = [((2 * a1 + z0) * 4, 2 * (2 * a2 + core)) for a1, a2 in places]
+        for number in range(16):
+            turn, round_ = number % 2, number // 2
+            x, c = x_out[(round_ + 2 * turn) % 4], (round_ + round_ // 4 + turn) % 2
+            to_bx, to_by = places[turn][0] + x, places[turn][1] + c
+            src, dst = obuf.at[boxes[turn], i, x, c], orecv.at[chip]
+            here = jnp.logical_and(to_bx == bx, to_by == by)
+
+            @pl.when(here)
+            def _(src=src, dst=dst):
+                pltpu.make_async_copy(src, dst, out_recv.at[2 * half + i]).start()
+
+            @pl.when(jnp.logical_not(here))
+            def _(src=src, dst=dst, to_bx=to_bx, to_by=to_by):
+                pltpu.make_async_remote_copy(
+                    src_ref=src, dst_ref=dst, send_sem=out_send, recv_sem=out_recv.at[2 * half + i],
+                    device_id=(to_bx, to_by), device_id_type=MESH,
+                ).start()
 
     def two_boxes(half, carry):
         level1(half, 1)
@@ -501,18 +518,14 @@
 
         def both_z(i, carry):
             level23(half, i)
-
-            def send_some(number, carry):
-                send_out(half, i, number)
-                return carry
-
-            lax.fori_loop(0, 16, send_some, 0)
+            send_out(half, i)
             return carry
 
         lax.fori_loop(0, 2, both_z, 0)
 
         @pl.when(half == 0)
         def _():
+            fill23(1)
             for phases in (phases2, phases3):
                 lax.fori_loop(2, 4, phases, 0)
 
@@ -561,6 +574,7 @@
     dense = (ROWS, LANES)
     scratch = [pltpu.VMEM(operands[i].shape, jnp.float32) for i in range(2)]
     scratch += [pltpu.VMEM((12, 2 * TERMS, DEPTH), jnp.bfloat16), pltpu.VMEM((4, 2 * TERMS, DEPTH), jnp.float32)]
+    scratch += [pltpu.VMEM((4, 96, 3 * LANES), jnp.bfloat16)]
     scratch += [
         pltpu.VMEM(shape, jnp.float32)
         for shape in (
@@ -570,7 +584,7 @@
             (4, 2, 2, 4) + dense,
             (4, 2, 2, 4, 40, LANES),
             (2, 2, 4) + dense,
-            (4, 2, 2, 2, 2) + dense,
+            (4, 2, 4, 2) + dense,
             (64,) + dense,
             (29, TERMS, LANES),
             (32, 4, 2, TERMS, LANES),

time: 76.7 us -> 77.2 us (level)
  no operation moved by 1% of the time
where the time goes in v10:
time: 77.2 us; the launch traced here: 77.1 us
  Pallas kernels  75.7 us (98%)
  local copies, waits for them, and re-layouts  1.41 us (2%)
    pallas_call x1, Pallas kernels, shards(): pl.pallas_call(kernel, out_shape=jax.ShapeDtypeStruct((ROWS * 64, LANES),...  75.7 us

profile of v10, /device:TPU:1, one launch (start us, length us, event | category | flops | bytes accessed | tf_op | source)
XLA Modules:
  0.0 77.1 jit_solution(1958744174690866790)
XLA Ops:
  0.0 75.7 %shard_map.28 = f32[4608,128]{1,0:T(8,128)S(1)} custom-call(f32[4608,128]{1,0:T(8,128)} %bitcast.7, f32[4,96,96]{2,1,0:T(8,128)} %slow_hbm.1), custom_call_target="tpu_custom_call" | custom-call | tf_op jit(solution)/shard_map/pallas_call | solution.py:606
  75.7 1.4 %copy.4 = f32[2,6,64,6,128]{4,2,3,1,0:T(8,128)} copy(f32[2,6,64,6,128]{4,2,3,1,0:T(8,128)S(1)} %bitcast.6) | data formatting | bytes 4718592

commit v11 on v10

--- a/solution.py
+++ b/solution.py
@@ -35,6 +35,20 @@
 WHOLE = 1.5 * 2.0**23
 
 
+RESULT_ORDER = (
+    (
+        (0, 0, 1), (1, 2, 0), (0, 1, 0), (1, 3, 1),
+        (0, 2, 1), (1, 0, 0), (0, 3, 0), (1, 1, 1),
+        (0, 2, 0), (1, 0, 1), (0, 3, 1), (1, 1, 0),
+        (0, 0, 0), (1, 2, 1), (0, 1, 1), (1, 3, 0),
+    ),
+    (
+        (1, 3, 0), (0, 1, 1), (0, 2, 0), (1, 0, 1),
+        (0, 0, 0), (1, 2, 1), (0, 3, 1), (1, 1, 0),
+        (0, 2, 1), (1, 0, 0), (0, 1, 0), (1, 3, 1),
+        (0, 0, 1), (1, 2, 0), (0, 3, 0), (1, 1, 1),
+    ),
+)
 POINTS = [float(point) for point in cheb_points()]
 SCALES = [
     float(1 / np.prod([cheb_points()[s] - cheb_points()[j] for j in range(CHEB) if j != s])) for s in range(CHEB)
@@ -486,18 +500,23 @@
                         obuf[box, i, 2 * x1 + q1, 0, rows, :] = jnp.where(left_half, upper, pltpu.roll(lower, 64, 1))
                         obuf[box, i, 2 * x1 + q1, 1, rows, :] = jnp.where(left_half, pltpu.roll(upper, 64, 1), lower)
 
-    x_out = [lax.rem(my_x + 1 + 2 * core + k, 4) for k in range(4)]
+    x_out = [lax.rem(my_x + k, 4) for k in range(4)]
+    role = lax.rem(core + my_y, 2)
+
+    def by_role(first, second):
+        return first if first is second else first + role * (second - first)
 
     def send_out(half, i):
-        boxes = [2 * half + core, 2 * half + 1 - core]
+        boxes = [2 * half + side for side in range(2)]
         z0 = lax.rem(my_z + i, 2)
         places = [box_of(box) for box in boxes]
         places = [((2 * a1 + z0) * 4, 2 * (2 * a2 + core)) for a1, a2 in places]
-        for number in range(16):
-            turn, round_ = number % 2, number // 2
-            x, c = x_out[(round_ + 2 * turn) % 4], (round_ + round_ // 4 + turn) % 2
-            to_bx, to_by = places[turn][0] + x, places[turn][1] + c
-            src, dst = obuf.at[boxes[turn], i, x, c], orecv.at[chip]
+        for (side0, x0, c0), (side1, x1, c1) in zip(*RESULT_ORDER):
+            box = by_role(boxes[side0], boxes[side1])
+            to_z, to_y = [by_role(*ends) for ends in zip(places[side0], places[side1])]
+            x, c = by_role(x_out[x0], x_out[x1]), c0 if c0 == c1 else by_role(c0, c1)
+            to_bx, to_by = to_z + x, to_y + c
+            src, dst = obuf.at[box, i, x, c], orecv.at[chip]
             here = jnp.logical_and(to_bx == bx, to_by == by)
 
             @pl.when(here)

time: 77.2 us -> 77.6 us (level)
  no operation moved by 1% of the time
where the time goes in v11:
time: 77.6 us; the launch traced here: 77.5 us
  Pallas kernels  76.1 us (98%)
  local copies, waits for them, and re-layouts  1.41 us (2%)
    pallas_call x1, Pallas kernels, shards(): pl.pallas_call(kernel, out_shape=jax.ShapeDtypeStruct((ROWS * 64, LANES),...  76.1 us

profile of v11, /device:TPU:1, one launch (start us, length us, event | category | flops | bytes accessed | tf_op | source)
XLA Modules:
  0.0 77.5 jit_solution(7266325235533004132)
XLA Ops:
  0.0 76.1 %shard_map.28 = f32[4608,128]{1,0:T(8,128)S(1)} custom-call(f32[4608,128]{1,0:T(8,128)} %bitcast.7, f32[4,96,96]{2,1,0:T(8,128)} %slow_hbm.1), custom_call_target="tpu_custom_call" | custom-call | tf_op jit(solution)/shard_map/pallas_call | solution.py:625
  76.1 1.4 %copy.4 = f32[2,6,64,6,128]{4,2,3,1,0:T(8,128)} copy(f32[2,6,64,6,128]{4,2,3,1,0:T(8,128)S(1)} %bitcast.6) | data formatting | bytes 4718592

commit v12 on v10

--- a/solution.py
+++ b/solution.py
@@ -17,6 +17,7 @@
 DEPTH = 256
 LANES = 128
 MESH = pl.DeviceIdType.MESH
+PIECES = (pl.ds(0, 40), pl.ds(40, 32))
 
 
 def cheb_points():
@@ -201,10 +202,11 @@
 
             @pl.when(jnp.logical_not(here))
             def _(src=src, dst=dst, to_bx=to_bx, to_by=to_by):
-                pltpu.make_async_remote_copy(
-                    src_ref=src, dst_ref=dst, send_sem=in_send, recv_sem=in_recv.at[part],
-                    device_id=(to_bx, to_by), device_id_type=MESH,
-                ).start()
+                for rows in PIECES:
+                    pltpu.make_async_remote_copy(
+                        src_ref=src.at[rows], dst_ref=dst.at[rows], send_sem=in_send, recv_sem=in_recv.at[part],
+                        device_id=(to_bx, to_by), device_id_type=MESH,
+                    ).start()
 
         @pl.when(part < 3)
         def _():
@@ -506,10 +508,11 @@
 
             @pl.when(jnp.logical_not(here))
             def _(src=src, dst=dst, to_bx=to_bx, to_by=to_by):
-                pltpu.make_async_remote_copy(
-                    src_ref=src, dst_ref=dst, send_sem=out_send, recv_sem=out_recv.at[2 * half + i],
-                    device_id=(to_bx, to_by), device_id_type=MESH,
-                ).start()
+                for rows in PIECES:
+                    pltpu.make_async_remote_copy(
+                        src_ref=src.at[rows], dst_ref=dst.at[rows], send_sem=out_send, recv_sem=out_recv.at[2 * half + i],
+                        device_id=(to_bx, to_by), device_id_type=MESH,
+                    ).start()
 
     def two_boxes(half, carry):
         level1(half, 1)

time: 77.2 us -> 77 us (level)
  no operation moved by 1% of the time
where the time goes in v12:
time: 77 us; the launch traced here: 76.9 us
  Pallas kernels  75.5 us (98%)
  local copies, waits for them, and re-layouts  1.41 us (2%)
    pallas_call x1, Pallas kernels, shards(): pl.pallas_call(kernel, out_shape=jax.ShapeDtypeStruct((ROWS * 64, LANES),...  75.5 us

profile of v12, /device:TPU:1, one launch (start us, length us, event | category | flops | bytes accessed | tf_op | source)
XLA Modules:
  0.0 76.9 jit_solution(3656899535589914394)
XLA Ops:
  0.0 75.5 %shard_map.28 = f32[4608,128]{1,0:T(8,128)S(1)} custom-call(f32[4608,128]{1,0:T(8,128)} %bitcast.7, f32[4,96,96]{2,1,0:T(8,128)} %slow_hbm.1), custom_call_target="tpu_custom_call" | custom-call | tf_op jit(solution)/shard_map/pallas_call | solution.py:609
  75.5 1.4 %copy.4 = f32[2,6,64,6,128]{4,2,3,1,0:T(8,128)} copy(f32[2,6,64,6,128]{4,2,3,1,0:T(8,128)S(1)} %bitcast.6) | data formatting | bytes 4718592
